TPU v7x, 128 devices: a whole 4x4x4 slice. The times are simulated.
128 devices in a mesh: gx: 4 (over y), gy: 32 (over z, x, core).
Axes of the slice: x: 4, y: 4, z: 4, core: 2. Of those that a mesh axis runs over, the one named last changes fastest.
Arguments:
- potential_heat_value: float32 [8, 1024, 4096], P(None, ('gx', 'gy')), may hold values from -6 to 6
- saltiness_anomaly: float32 [8, 1024, 4096], P(None, ('gx', 'gy')), may hold values from -6 to 6
- zonal_current_rate: float32 [8, 1024, 4096], P(None, ('gx', 'gy')), may hold values from -0.45 to 0.45
- meridional_current_rate: float32 [8, 1024, 4096], P(None, ('gx', 'gy')), may hold values from -0.45 to 0.45
- interface_mixing_factor: float32 [7, 1024, 4096], P(None, ('gx', 'gy')), may hold values from 0.1 to 10
- free_surface_diagonal_term: float32 [1024, 4096], P(('gx', 'gy')), may hold values from 0.02 to 0.5
- surface_drive_source: float32 [1024, 4096], P(('gx', 'gy')), may hold values from -6 to 6
- ocean_patch_flags: int32 [1024], replicated, may hold values from 0 to 1, as said below
- adjacent_patch_indices: int32 [1024, 8], replicated, may hold values from -1 to 1023, as said below
Outputs:
- temperature_next: float32 [8, 1024, 4096], P(None, ('gx', 'gy'))
- salinity_next: float32 [8, 1024, 4096], P(None, ('gx', 'gy'))
- zonal_next: float32 [8, 1024, 4096], P(None, ('gx', 'gy'))
- meridional_next: float32 [8, 1024, 4096], P(None, ('gx', 'gy'))
- surface_height: float32 [1024, 4096], P(('gx', 'gy'))
Inputs may be any that keep to these rules, and one draw needn't show every extreme that they name: `ocean_patch_flags`: block numbers run along the curve, 8 consecutive blocks on each device of gx+gy in order; devices 2j and 2j+1 together hold exactly 8 ocean blocks, and device 0 holds 8. `adjacent_patch_indices`: row b lists the neighbours of block b on a grid of 4 x 256 blocks, periodic east-west and closed north and south; -1 where there is none or it is land, and -1 throughout for a land block. The relation is symmetric, and a listed number differs from b by at most 7 counted around the 1024 numbers.
All inputs are finite; a program needn't handle non-finite values.
Results may differ from a plain program's by a relative error of at most 0.0001.
Values sent between devices are 32-bit elements; how exact they have to be, the bound alone decides.
A program may use at most 128 MiB of HBM per device.

v0:
```python
import jax
import jax.numpy as jnp
from jax import lax
from jax.sharding import PartitionSpec as P

BSIDE = 64
ITERS = 4


def swapped(block, axis, distance):
    count = lax.axis_size(axis)
    route = []
    for low in range(count):
        high = low | 1 << distance
        if high != low and high < count:
            route += [(low, high), (high, low)]
    return lax.ppermute(block, axis, route)


def passed_along(value, axis, steps):
    count = lax.axis_size(axis)
    pairs = [(source, (source + steps) % count) for source in range(count)]
    return lax.ppermute(value, axis, pairs)


def edge_strips(values, with_corners):
    square = values.reshape(values.shape[:-1] + (BSIDE, BSIDE))
    pieces = [square[..., :, -1], square[..., :, 0], square[..., -1, :], square[..., 0, :]]
    if with_corners:
        pieces = pieces + [
            square[..., -1, -1:],
            square[..., -1, :1],
            square[..., 0, -1:],
            square[..., 0, :1],
        ]
    return jnp.concatenate(pieces, axis=-1)


def pick_borders(strips, source, present):

    def picked(column, start, length):
        taken = jnp.take(strips, source[:, column], axis=-2)[..., start : start + length]
        return jnp.where(present[:, column : column + 1], taken, 0.0)

    borders = [
        picked(0, BSIDE, BSIDE),
        picked(1, 0, BSIDE),
        picked(2, 3 * BSIDE, BSIDE),
        picked(3, 2 * BSIDE, BSIDE),
    ]
    if strips.shape[-1] > 4 * BSIDE:
        borders = borders + [
            picked(4, 4 * BSIDE + 3, 1),
            picked(5, 4 * BSIDE + 2, 1),
            picked(6, 4 * BSIDE + 1, 1),
            picked(7, 4 * BSIDE, 1),
        ]
    return borders


def cell_positions(length):
    indices = jnp.arange(length)
    return (indices % BSIDE, indices // BSIDE)


def across(border):
    return jnp.tile(border, (1,) * (border.ndim - 1) + (BSIDE,))


def along_rows(border):
    return jnp.repeat(border, BSIDE, axis=-1)


def adjacent(values, borders):
    col_index, row_index = cell_positions(values.shape[-1])
    east_side = jnp.where(
        col_index == BSIDE - 1, along_rows(borders[0]), jnp.roll(values, -1, axis=-1)
    )
    west_side = jnp.where(col_index == 0, along_rows(borders[1]), jnp.roll(values, 1, axis=-1))
    north_side = jnp.where(
        row_index == BSIDE - 1, across(borders[2]), jnp.roll(values, -BSIDE, axis=-1)
    )
    south_side = jnp.where(row_index == 0, across(borders[3]), jnp.roll(values, BSIDE, axis=-1))
    return (east_side, west_side, north_side, south_side)


def upwind(carried_quantity, zonal, meridional, beside):
    east_side, west_side, north_side, south_side = beside
    across_x = jnp.maximum(zonal, 0.0) * (carried_quantity - west_side) + jnp.minimum(
        zonal, 0.0
    ) * (east_side - carried_quantity)
    across_y = jnp.maximum(meridional, 0.0) * (carried_quantity - south_side) + jnp.minimum(
        meridional, 0.0
    ) * (north_side - carried_quantity)
    return carried_quantity - across_x - across_y


def nine_point(values, diagonal, borders):
    east_side, west_side, north_side, south_side = adjacent(values, borders)
    col_index, row_index = cell_positions(values.shape[-1])
    paired = east_side + west_side
    north_line = jnp.concatenate([borders[2][..., 1:], borders[4]], axis=-1) + jnp.concatenate(
        [borders[5], borders[2][..., :-1]], axis=-1
    )
    south_line = jnp.concatenate([borders[3][..., 1:], borders[6]], axis=-1) + jnp.concatenate(
        [borders[7], borders[3][..., :-1]], axis=-1
    )
    upper = jnp.where(row_index == BSIDE - 1, across(north_line), jnp.roll(paired, -BSIDE, axis=-1))
    lower = jnp.where(row_index == 0, across(south_line), jnp.roll(paired, BSIDE, axis=-1))
    return (
        (6.0 + diagonal) * values
        - (east_side + west_side + north_side + south_side)
        - 0.5 * (upper + lower)
    )


def vertical_mix(values, interface_mixing_factor):
    levels = values.shape[0]
    factors = []
    carried = []
    for level in range(levels):
        lower_rate = interface_mixing_factor[level - 1] if level > 0 else 0.0
        upper_rate = interface_mixing_factor[level] if level < levels - 1 else 0.0
        pivot = 1.0 + lower_rate + upper_rate
        right_side = values[level]
        if level > 0:
            pivot = pivot - lower_rate * factors[-1]
            right_side = right_side + lower_rate * carried[-1]
        factors.append(upper_rate / pivot)
        carried.append(right_side / pivot)
    solved = [carried[-1]]
    for level in range(levels - 2, -1, -1):
        solved.insert(0, carried[level] + factors[level] * solved[0])
    return jnp.stack(solved)


def pair_swap(payload):
    return swapped(payload, ("gx", "gy"), 0)


def squared_norm(residual, scaled):
    return lax.psum(jnp.sum(residual * scaled), ("gx", "gy"))


def conjugate(surface_load, centre, operator):
    height = jnp.zeros_like(surface_load)
    residual = surface_load
    scaled = residual / centre
    direction = scaled
    current = squared_norm(residual, scaled)
    for iteration in range(ITERS):
        image = operator(direction)
        alpha_step = current / lax.psum(jnp.sum(direction * image), ("gx", "gy"))
        height = height + alpha_step * direction
        residual = residual - alpha_step * image
        if iteration + 1 < ITERS:
            scaled = residual / centre
            following = squared_norm(residual, scaled)
            direction = scaled + following / current * direction
            current = following
    return height


def local(
    potential_heat_value,
    saltiness_anomaly,
    zonal_current_rate,
    meridional_current_rate,
    interface_mixing_factor,
    free_surface_diagonal_term,
    surface_drive_source,
    ocean_patch_flags,
    adjacent_patch_indices,
):
    devices = lax.axis_size(("gx", "gy"))
    position = lax.axis_index(("gx", "gy"))
    patch_pieces_grid = potential_heat_value.shape[1]
    half_blocks = patch_pieces_grid // 2
    total_blocks = patch_pieces_grid * devices
    ocean_flags = (ocean_patch_flags > 0).astype(jnp.int32)
    own_ocean = lax.dynamic_slice_in_dim(
        ocean_flags, position * patch_pieces_grid, patch_pieces_grid
    )
    weight = own_ocean.astype(jnp.float32)[:, None]
    own_lists = lax.dynamic_slice_in_dim(
        adjacent_patch_indices, position * patch_pieces_grid, patch_pieces_grid, 0
    )
    present = own_lists >= 0
    source = jnp.where(
        present, jnp.mod(own_lists - (position - 1) * patch_pieces_grid, total_blocks), 0
    )
    carried_quantities = (
        potential_heat_value,
        saltiness_anomaly,
        zonal_current_rate,
        meridional_current_rate,
    )
    strips = jnp.stack(
        [edge_strips(carried_quantity, False) for carried_quantity in carried_quantities]
    )
    arrived = [passed_along(strips, ("gx", "gy"), offset) for offset in (1, -1)]
    window = jnp.concatenate([arrived[0], strips, arrived[1]], axis=-2)
    borders = pick_borders(window, source, present)
    mixed_fields = []
    for number, carried_quantity in enumerate(carried_quantities):
        beside = adjacent(carried_quantity, [border[number] for border in borders])
        advected = upwind(carried_quantity, zonal_current_rate, meridional_current_rate, beside)
        mixed_fields.append(vertical_mix(advected, interface_mixing_factor))
    surface_load = (
        surface_drive_source + jnp.mean(mixed_fields[0] - mixed_fields[1], axis=0)
    ) * weight
    ocean_rank = jnp.cumsum(ocean_flags) - ocean_flags
    own_rank = lax.dynamic_slice_in_dim(ocean_rank, position * patch_pieces_grid, patch_pieces_grid)
    pair_base = position // 2 * 2
    pair_ocean = lax.dynamic_slice_in_dim(
        ocean_flags, pair_base * patch_pieces_grid, 2 * patch_pieces_grid
    )
    pair_rank = lax.dynamic_slice_in_dim(
        ocean_rank, pair_base * patch_pieces_grid, 2 * patch_pieces_grid
    )
    slot_rank = position * half_blocks + jnp.arange(half_blocks, dtype=jnp.int32)
    matches = (pair_rank[None, :] == slot_rank[:, None]) & (pair_ocean[None, :] > 0)
    pair_slot = jnp.sum(
        jnp.where(matches, jnp.arange(2 * patch_pieces_grid, dtype=jnp.int32)[None, :], 0), axis=1
    )
    from_self = pair_slot // patch_pieces_grid == position - pair_base
    within = pair_slot % patch_pieces_grid
    payload = jnp.stack([surface_load, free_surface_diagonal_term])
    incoming = pair_swap(payload)
    combined = jnp.concatenate([payload, incoming], axis=1)
    tropic = jnp.take(combined, jnp.where(from_self, within, patch_pieces_grid + within), axis=1)
    tropic_load = tropic[0]
    tropic_diagonal = tropic[1]
    slot_block = pair_base * patch_pieces_grid + pair_slot
    slot_lists = jnp.take(adjacent_patch_indices, slot_block, axis=0)
    slot_present = slot_lists >= 0
    slot_target = jnp.take(ocean_rank, jnp.maximum(slot_lists, 0))
    slot_source = jnp.where(
        slot_present, jnp.mod(slot_target - (position - 2) * half_blocks, half_blocks * devices), 0
    )

    def tropic_borders(values, with_corners):
        strips_here = edge_strips(values, with_corners)
        arrived_here = [
            passed_along(strips_here, ("gx", "gy"), offset) for offset in (2, 1, -1, -2)
        ]
        window_here = jnp.concatenate(
            [arrived_here[0], arrived_here[1], strips_here, arrived_here[2], arrived_here[3]],
            axis=-2,
        )
        return pick_borders(window_here, slot_source, slot_present)

    def tropic_operator(direction):
        return nine_point(direction, tropic_diagonal, tropic_borders(direction, True))

    height = conjugate(tropic_load, 6.0 + tropic_diagonal, tropic_operator)
    beside = adjacent(height, tropic_borders(height, False))
    package = jnp.stack([height, 0.5 * (beside[0] - beside[1]), 0.5 * (beside[2] - beside[3])])
    returned = pair_swap(package)
    target_device = own_rank // half_blocks
    back_index = jnp.where(
        own_ocean > 0,
        own_rank % half_blocks + half_blocks * (target_device != position).astype(jnp.int32),
        0,
    )
    result = jnp.take(jnp.concatenate([package, returned], axis=1), back_index, axis=1)
    return (
        mixed_fields[0] * weight,
        mixed_fields[1] * weight,
        (mixed_fields[2] - result[1]) * weight,
        (mixed_fields[3] - result[2]) * weight,
        result[0] * weight,
    )


def solution(mesh):
    return jax.shard_map(
        local,
        mesh=mesh,
        in_specs=(
            P(None, ("gx", "gy"), None),
            P(None, ("gx", "gy"), None),
            P(None, ("gx", "gy"), None),
            P(None, ("gx", "gy"), None),
            P(None, ("gx", "gy"), None),
            P(("gx", "gy"), None),
            P(("gx", "gy"), None),
            P(),
            P(),
        ),
        out_specs=(
            P(None, ("gx", "gy"), None),
            P(None, ("gx", "gy"), None),
            P(None, ("gx", "gy"), None),
            P(None, ("gx", "gy"), None),
            P(("gx", "gy"), None),
        ),
        check_vma=False,
    )
```

profile of v0, /device:TPU:0, one launch (start us, length us, event | category | flops | bytes accessed | tf_op | source)
XLA Modules:
  0.0 826.1 jit_solution(7734730557891944791)
XLA Ops:
  8.4 5.1 fusion.251
  16.4 5.0 fusion.253
  25.3 5.0 fusion.255
  52.1 19.6 %collective-permute-start.1 = (f32[4,8,8,256]{3,1,2,0:T(8,128)}, f32[4,8,8,256]{3,1,2,0:T(8,128)}, u32[]{:S(2)}, u32[]{:S(2)}) collective-permute-start(f32[4,8,8,256]{3,1,2,0:T(8,128)} %pad_maximum_fusion.3), channel_id=1, source_target_pairs={{0,127},{1,0},{2,1},{3,2},{4,3},{5,4},{6,5},{7,6},{8,7},{9,8},{10,... | collective-permute-start | bytes 786440 | tf_op jit(solution)/shard_map/ppermute | solution.py:23
  116.8 2.9 reshape.2285
  124.5 2.9 tile.268
  132.3 2.9 tile.271
  140.5 3.0 reshape.2284
  145.5 2.9 reshape.2309
  149.9 2.9 tile.334
  154.3 2.9 tile.337
  159.2 2.9 reshape.2308
  164.1 2.9 reshape.2287
  168.5 3.0 tile.274
  173.0 2.9 tile.277
  177.9 3.3 reshape.2286
  181.3 4.7 fusion.40
  208.1 2.9 tile.283
  213.8 3.0 reshape.2288
  216.9 4.7 fusion.28
  233.3 7.0 collective-permute-start.5
  255.5 63.9 %all-reduce = (f32[]{:T(128)}, f32[]{:T(128)}) all-reduce(f32[]{:T(128)} %get-tuple-element.9, f32[]{:T(128)} %get-tuple-element.8), channel_id=1, replica_groups=mesh['gx'=4,'gy'=32] {'gx','gy'}, use_global_device_ids=true, to_apply=%region_5.7 | all-reduce | flops 2 | bytes 16 | tf_op jit(solution)/shard_map/psum | solution.py:142
  321.4 64.5 %psum.58 = f32[]{:T(128)} all-reduce(f32[]{:T(128)} %get-tuple-element.74), channel_id=1, replica_groups=mesh['gx'=4,'gy'=32] {'gx','gy'}, use_global_device_ids=true, to_apply=%region_9.12 | all-reduce | flops 1 | bytes 8 | tf_op jit(solution)/shard_map/psum | solution.py:142
  391.4 7.2 collective-permute-start.9
  419.3 62.5 %psum.59 = f32[]{:T(128)} all-reduce(f32[]{:T(128)} %get-tuple-element.63), channel_id=1, replica_groups=mesh['gx'=4,'gy'=32] {'gx','gy'}, use_global_device_ids=true, to_apply=%region_11.14 | all-reduce | flops 1 | bytes 8 | tf_op jit(solution)/shard_map/psum | solution.py:153
  484.6 62.0 %psum.60 = f32[]{:T(128)} all-reduce(f32[]{:T(128)} %get-tuple-element.61), channel_id=1, replica_groups=mesh['gx'=4,'gy'=32] {'gx','gy'}, use_global_device_ids=true, to_apply=%region_13.16 | all-reduce | flops 1 | bytes 8 | tf_op jit(solution)/shard_map/psum | solution.py:142
  553.9 7.2 collective-permute-start.13
  581.2 62.4 %psum.61 = f32[]{:T(128)} all-reduce(f32[]{:T(128)} %get-tuple-element.50), channel_id=1, replica_groups=mesh['gx'=4,'gy'=32] {'gx','gy'}, use_global_device_ids=true, to_apply=%region_15.18 | all-reduce | flops 1 | bytes 8 | tf_op jit(solution)/shard_map/psum | solution.py:153
  646.4 62.9 %psum.62 = f32[]{:T(128)} all-reduce(f32[]{:T(128)} %multiply_reduce_fusion), channel_id=1, replica_groups=mesh['gx'=4,'gy'=32] {'gx','gy'}, use_global_device_ids=true, to_apply=%region_17.20 | all-reduce | flops 1 | bytes 8 | tf_op jit(solution)/shard_map/psum | solution.py:142
  716.8 7.2 collective-permute-start.17
  738.4 63.2 %psum.63 = f32[]{:T(128)} all-reduce(f32[]{:T(128)} %fusion.155), channel_id=1, replica_groups=mesh['gx'=4,'gy'=32] {'gx','gy'}, use_global_device_ids=true, to_apply=%region_19.22 | all-reduce | flops 1 | bytes 8 | tf_op jit(solution)/shard_map/psum | solution.py:153
  803.9 7.2 collective-permute-start.21
  (810 shorter events, 250.6 us)
Async XLA Ops:
  52.1 57.5 %collective-permute-start = (f32[4,8,8,256]{3,1,2,0:T(8,128)}, f32[4,8,8,256]{3,1,2,0:T(8,128)}, u32[]{:S(2)}, u32[]{:S(2)}) collective-permute-start(f32[4,8,8,256]{3,1,2,0:T(8,128)} %pad_maximum_fusion.3), channel_id=1, source_target_pairs={{0,1},{1,2},{2,3},{3,4},{4,5},{5,6},{6,7},{7,8},{8,9},{9,10},{10,1... | collective-permute-start | bytes 786440 | tf_op jit(solution)/shard_map/ppermute | solution.py:23
  52.1 57.5 %collective-permute-start.1 = (f32[4,8,8,256]{3,1,2,0:T(8,128)}, f32[4,8,8,256]{3,1,2,0:T(8,128)}, u32[]{:S(2)}, u32[]{:S(2)}) collective-permute-start(f32[4,8,8,256]{3,1,2,0:T(8,128)} %pad_maximum_fusion.3), channel_id=1, source_target_pairs={{0,127},{1,0},{2,1},{3,2},{4,3},{5,4},{6,5},{7,6},{8,7},{9,8},{10,... | collective-permute-start | bytes 786440 | tf_op jit(solution)/shard_map/ppermute | solution.py:23
  229.0 1.6 collective-permute-start.2
  233.0 12.0 %collective-permute-start.3 = (f32[4,260]{1,0:T(4,128)S(1)}, f32[4,260]{1,0:T(4,128)S(1)}, u32[]{:S(2)}, u32[]{:S(2)}) collective-permute-start(f32[4,260]{1,0:T(4,128)S(1)} %concatenate.635), channel_id=1, source_target_pairs={{0,2},{1,3},{2,4},{3,5},{4,6},{5,7},{6,8},{7,9},{8,10},{9,11},{10,... | collective-permute-start | bytes 12488 | tf_op jit(solution)/shard_map/ppermute | solution.py:23
  233.1 12.0 %collective-permute-start.4 = (f32[4,260]{1,0:T(4,128)S(1)}, f32[4,260]{1,0:T(4,128)S(1)}, u32[]{:S(2)}, u32[]{:S(2)}) collective-permute-start(f32[4,260]{1,0:T(4,128)S(1)} %concatenate.635), channel_id=1, source_target_pairs={{0,1},{1,2},{2,3},{3,4},{4,5},{5,6},{6,7},{7,8},{8,9},{9,10},{10,1... | collective-permute-start | bytes 12488 | tf_op jit(solution)/shard_map/ppermute | solution.py:23
  233.3 11.8 %collective-permute-start.5 = (f32[4,260]{1,0:T(4,128)S(1)}, f32[4,260]{1,0:T(4,128)S(1)}, u32[]{:S(2)}, u32[]{:S(2)}) collective-permute-start(f32[4,260]{1,0:T(4,128)S(1)} %concatenate.635), channel_id=1, source_target_pairs={{0,127},{1,0},{2,1},{3,2},{4,3},{5,4},{6,5},{7,6},{8,7},{9,8},{10,... | collective-permute-start | bytes 12488 | tf_op jit(solution)/shard_map/ppermute | solution.py:23
  240.3 4.7 collective-permute-start.6
  250.3 137.2 %copy-start.65 = (pred[64,64]{1,0:T(8,128)(4,1)S(1)}, pred[64,64]{1,0:T(8,128)(4,1)}, u32[]{:S(2)}) copy-start(pred[64,64]{1,0:T(8,128)(4,1)} %get-tuple-element.420) | copy-start | bytes 12292
  250.3 137.2 %copy-start.66 = (pred[64,64]{1,0:T(8,128)(4,1)S(1)}, pred[64,64]{1,0:T(8,128)(4,1)}, u32[]{:S(2)}) copy-start(pred[64,64]{1,0:T(8,128)(4,1)} %get-tuple-element.421) | copy-start | bytes 12292
  250.3 137.2 %copy-start.67 = (pred[64,64]{1,0:T(8,128)(4,1)S(1)}, pred[64,64]{1,0:T(8,128)(4,1)}, u32[]{:S(2)}) copy-start(pred[64,64]{1,0:T(8,128)(4,1)} %get-tuple-element.422) | copy-start | bytes 12292
  250.3 137.2 %copy-start.68 = (pred[64,64]{1,0:T(8,128)(4,1)S(1)}, pred[64,64]{1,0:T(8,128)(4,1)}, u32[]{:S(2)}) copy-start(pred[64,64]{1,0:T(8,128)(4,1)} %get-tuple-element.423) | copy-start | bytes 12292
  388.9 17.0 %collective-permute-start.10 = (f32[4,260]{1,0:T(4,128)S(1)}, f32[4,260]{1,0:T(4,128)S(1)}, u32[]{:S(2)}, u32[]{:S(2)}) collective-permute-start(f32[4,260]{1,0:T(4,128)S(1)} %concatenate.653), channel_id=1, source_target_pairs={{0,126},{1,127},{2,0},{3,1},{4,2},{5,3},{6,4},{7,5},{8,6},{9,7},{1... | collective-permute-start | bytes 12488 | tf_op jit(solution)/shard_map/ppermute | solution.py:23
  390.6 15.3 %collective-permute-start.7 = (f32[4,260]{1,0:T(4,128)S(1)}, f32[4,260]{1,0:T(4,128)S(1)}, u32[]{:S(2)}, u32[]{:S(2)}) collective-permute-start(f32[4,260]{1,0:T(4,128)S(1)} %concatenate.653), channel_id=1, source_target_pairs={{0,2},{1,3},{2,4},{3,5},{4,6},{5,7},{6,8},{7,9},{8,10},{9,11},{10,... | collective-permute-start | bytes 12488 | tf_op jit(solution)/shard_map/ppermute | solution.py:23
  391.4 14.5 %collective-permute-start.8 = (f32[4,260]{1,0:T(4,128)S(1)}, f32[4,260]{1,0:T(4,128)S(1)}, u32[]{:S(2)}, u32[]{:S(2)}) collective-permute-start(f32[4,260]{1,0:T(4,128)S(1)} %concatenate.653), channel_id=1, source_target_pairs={{0,1},{1,2},{2,3},{3,4},{4,5},{5,6},{6,7},{7,8},{8,9},{9,10},{10,1... | collective-permute-start | bytes 12488 | tf_op jit(solution)/shard_map/ppermute | solution.py:23
  391.4 14.5 %collective-permute-start.9 = (f32[4,260]{1,0:T(4,128)S(1)}, f32[4,260]{1,0:T(4,128)S(1)}, u32[]{:S(2)}, u32[]{:S(2)}) collective-permute-start(f32[4,260]{1,0:T(4,128)S(1)} %concatenate.653), channel_id=1, source_target_pairs={{0,127},{1,0},{2,1},{3,2},{4,3},{5,4},{6,5},{7,6},{8,7},{9,8},{10,... | collective-permute-start | bytes 12488 | tf_op jit(solution)/shard_map/ppermute | solution.py:23
  552.4 16.6 %collective-permute-start.11 = (f32[4,260]{1,0:T(4,128)S(1)}, f32[4,260]{1,0:T(4,128)S(1)}, u32[]{:S(2)}, u32[]{:S(2)}) collective-permute-start(f32[4,260]{1,0:T(4,128)S(1)} %concatenate.689), channel_id=1, source_target_pairs={{0,2},{1,3},{2,4},{3,5},{4,6},{5,7},{6,8},{7,9},{8,10},{9,11},{10,... | collective-permute-start | bytes 12488 | tf_op jit(solution)/shard_map/ppermute | solution.py:23
  553.9 15.2 %collective-permute-start.12 = (f32[4,260]{1,0:T(4,128)S(1)}, f32[4,260]{1,0:T(4,128)S(1)}, u32[]{:S(2)}, u32[]{:S(2)}) collective-permute-start(f32[4,260]{1,0:T(4,128)S(1)} %concatenate.689), channel_id=1, source_target_pairs={{0,1},{1,2},{2,3},{3,4},{4,5},{5,6},{6,7},{7,8},{8,9},{9,10},{10,1... | collective-permute-start | bytes 12488 | tf_op jit(solution)/shard_map/ppermute | solution.py:23
  553.9 15.2 %collective-permute-start.13 = (f32[4,260]{1,0:T(4,128)S(1)}, f32[4,260]{1,0:T(4,128)S(1)}, u32[]{:S(2)}, u32[]{:S(2)}) collective-permute-start(f32[4,260]{1,0:T(4,128)S(1)} %concatenate.689), channel_id=1, source_target_pairs={{0,127},{1,0},{2,1},{3,2},{4,3},{5,4},{6,5},{7,6},{8,7},{9,8},{10,... | collective-permute-start | bytes 12488 | tf_op jit(solution)/shard_map/ppermute | solution.py:23
  561.1 8.0 collective-permute-start.14
  715.9 13.3 %collective-permute-start.15 = (f32[4,260]{1,0:T(4,128)S(1)}, f32[4,260]{1,0:T(4,128)S(1)}, u32[]{:S(2)}, u32[]{:S(2)}) collective-permute-start(f32[4,260]{1,0:T(4,128)S(1)} %concatenate.725), channel_id=1, source_target_pairs={{0,2},{1,3},{2,4},{3,5},{4,6},{5,7},{6,8},{7,9},{8,10},{9,11},{10,... | collective-permute-start | bytes 12488 | tf_op jit(solution)/shard_map/ppermute | solution.py:23
  716.8 12.4 %collective-permute-start.16 = (f32[4,260]{1,0:T(4,128)S(1)}, f32[4,260]{1,0:T(4,128)S(1)}, u32[]{:S(2)}, u32[]{:S(2)}) collective-permute-start(f32[4,260]{1,0:T(4,128)S(1)} %concatenate.725), channel_id=1, source_target_pairs={{0,1},{1,2},{2,3},{3,4},{4,5},{5,6},{6,7},{7,8},{8,9},{9,10},{10,1... | collective-permute-start | bytes 12488 | tf_op jit(solution)/shard_map/ppermute | solution.py:23
  716.8 12.4 %collective-permute-start.17 = (f32[4,260]{1,0:T(4,128)S(1)}, f32[4,260]{1,0:T(4,128)S(1)}, u32[]{:S(2)}, u32[]{:S(2)}) collective-permute-start(f32[4,260]{1,0:T(4,128)S(1)} %concatenate.725), channel_id=1, source_target_pairs={{0,127},{1,0},{2,1},{3,2},{4,3},{5,4},{6,5},{7,6},{8,7},{9,8},{10,... | collective-permute-start | bytes 12488 | tf_op jit(solution)/shard_map/ppermute | solution.py:23
  724.0 5.2 collective-permute-start.18
  736.5 76.5 %copy-start.60 = (f32[1,4,4096]{2,1,0:T(4,128)S(1)}, f32[1,4,4096]{2,1,0:T(4,128)}, u32[]{:S(2)}) copy-start(f32[1,4,4096]{2,1,0:T(4,128)} %reshape.2297) | copy-start | bytes 196612
  736.5 76.6 %copy-start.61 = (f32[1,4,4096]{2,1,0:T(4,128)S(1)}, f32[1,4,4096]{2,1,0:T(4,128)}, u32[]{:S(2)}) copy-start(f32[1,4,4096]{2,1,0:T(4,128)} %tile.302) | copy-start | bytes 196612
  736.5 76.6 %copy-start.62 = (f32[1,4,4096]{2,1,0:T(4,128)S(1)}, f32[1,4,4096]{2,1,0:T(4,128)}, u32[]{:S(2)}) copy-start(f32[1,4,4096]{2,1,0:T(4,128)} %tile.300) | copy-start | bytes 196612
  736.5 76.6 %copy-start.152 = (f32[1,4,1]{2,1,0:T(4,128)S(1)}, f32[1,4,1]{2,1,0:T(4,128)}, u32[]{:S(2)}) copy-start(f32[1,4,1]{2,1,0:T(4,128)} %get-tuple-element.250) | copy-start | bytes 52
  803.5 12.1 %collective-permute-start.19 = (f32[4,256]{1,0:T(4,128)S(1)}, f32[4,256]{1,0:T(4,128)S(1)}, u32[]{:S(2)}, u32[]{:S(2)}) collective-permute-start(f32[4,256]{1,0:T(4,128)S(1)} %pad_maximum_fusion.24), channel_id=1, source_target_pairs={{0,2},{1,3},{2,4},{3,5},{4,6},{5,7},{6,8},{7,9},{8,10},{9,11},{10,... | collective-permute-start | bytes 12296 | tf_op jit(solution)/shard_map/ppermute | solution.py:23
  803.9 11.8 %collective-permute-start.20 = (f32[4,256]{1,0:T(4,128)S(1)}, f32[4,256]{1,0:T(4,128)S(1)}, u32[]{:S(2)}, u32[]{:S(2)}) collective-permute-start(f32[4,256]{1,0:T(4,128)S(1)} %pad_maximum_fusion.24), channel_id=1, source_target_pairs={{0,1},{1,2},{2,3},{3,4},{4,5},{5,6},{6,7},{7,8},{8,9},{9,10},{10,1... | collective-permute-start | bytes 12296 | tf_op jit(solution)/shard_map/ppermute | solution.py:23
  803.9 11.8 %collective-permute-start.21 = (f32[4,256]{1,0:T(4,128)S(1)}, f32[4,256]{1,0:T(4,128)S(1)}, u32[]{:S(2)}, u32[]{:S(2)}) collective-permute-start(f32[4,256]{1,0:T(4,128)S(1)} %pad_maximum_fusion.24), channel_id=1, source_target_pairs={{0,127},{1,0},{2,1},{3,2},{4,3},{5,4},{6,5},{7,6},{8,7},{9,8},{10,... | collective-permute-start | bytes 12296 | tf_op jit(solution)/shard_map/ppermute | solution.py:23
  811.0 4.6 collective-permute-start.22
  819.7 1.5 collective-permute-start.23
  (149 other events, 1322.4 us)
where the time goes:
time: 837 us; the launch traced here: 826 us
  blocking collectives  441 us (53%)
  local copies, waits for them, and re-layouts  240 us (29%)
  starting transfers between devices  66.4 us (8%)
  other arithmetic  62.6 us (7%)
  between operations  12.8 us (2%)
    psum x4, blocking collectives, squared_norm(): return lax.psum(jnp.sum(residual * scaled), ('gx', 'gy'))  253 us
    psum x3, blocking collectives, conjugate(): alpha_step = current / lax.psum(jnp.sum(direction * image), ('gx', 'gy'))  188 us
    ppermute x22, starting transfers between devices, passed_along(): return lax.ppermute(value, axis, pairs)  66.2 us
    another operation x74, local copies, waits for them, and re-layouts, across(): return jnp.tile(border, (1,) * (border.ndim - 1) + (BSIDE,))  49.2 us
    gather x40, local copies, waits for them, and re-layouts, picked(): jnp.take(strips, source[:, column], axis=-2)[..., start:start + length]  31.9 us
    reshape x24, local copies, waits for them, and re-layouts, along_rows(): return jnp.repeat(border, BSIDE, axis=-1)  29.3 us
    slice x6, local copies, waits for them, and re-layouts, edge_strips(): square[..., :, -1]  18.1 us
  transfers between devices with their start and end apart: 24, of which 2 were waited for; matrix products, arithmetic and copies ran while one was open for 7% of the time, Pallas kernels for 0%

commit v1 on v0

v1 whole, which is shorter than its diff:
```python
import functools

import jax
import jax.numpy as jnp
from jax import lax
from jax.experimental import pallas as pl
from jax.experimental.pallas import tpu as pltpu
from jax.sharding import PartitionSpec as P

MESH = pl.DeviceIdType.MESH
F32 = jnp.float32
LANES = 128
SLOTS = 8
LEVELS = 8
PAIRS = 32
CELLS = 4096
ROWS = 64
HALO = 4
NEAR = 8


def tile(t):
    return pl.ds(pl.multiple_of(t * LANES, LANES), LANES)


def kernel(
    sizes,
    t_in, s_in, u_in, v_in, k_in, c_in, g_in, flags, lists,
    t_out, s_out, u_out, v_out, sx_out, sy_out, h_out,
    q, kk, cc, src, own_lists, mixed, ip, fu, gl, hx,
    strips, arrived, mstrips, marrived, zstrips, zarrived,
    z2, mi2, zx, mx, mrow, vp, part, near_a, far_a, near_b, far_b,
    in_sem, out_sem, strip_send, strip_recv, m_send, m_recv, z_send, z_recv,
    near_send, near_recv, far_send, far_recv,
):
    count_x, count_y = sizes
    total = count_x * count_y
    gx, gy = lax.axis_index("gx"), lax.axis_index("gy")
    pos = gx * count_y + gy
    far_count = total // NEAR
    highs = count_y // NEAR
    low, high = gy % NEAR, gy // NEAR
    far_id = gx * highs + high
    before, after = (pos + total - 1) % total, (pos + 1) % total
    ring = [(before // count_y, before % count_y), (after // count_y, after % count_y)]
    near_peers = [(gx, high * NEAR + (low + r) % NEAR) for r in range(1, NEAR)]
    far_peers = []
    for r in range(1, far_count):
        other = (far_id + r) % far_count
        far_peers.append((other // highs, (other % highs) * NEAR + low))

    barrier = pltpu.get_barrier_semaphore()
    partners = ring + near_peers + far_peers
    for peer in partners:
        pl.semaphore_signal(barrier, inc=1, device_id=peer, device_id_type=MESH)

    loads = []
    for number, ref in enumerate((t_in, s_in, u_in, v_in)):
        loads.append(
            pltpu.make_async_copy(ref, q.at[number, :, pl.ds(LANES, CELLS)], in_sem.at[number])
        )
    loads.append(pltpu.make_async_copy(lists.at[pl.ds(pos * SLOTS, SLOTS)], own_lists, in_sem.at[4]))
    loads.append(pltpu.make_async_copy(c_in, cc, in_sem.at[5]))
    loads.append(pltpu.make_async_copy(k_in, kk, in_sem.at[6]))
    loads.append(pltpu.make_async_copy(g_in, src, in_sem.at[7]))
    for load in loads:
        load.start()

    lane = lax.broadcasted_iota(jnp.int32, (SLOTS, LANES), 1)
    slot = lax.broadcasted_iota(jnp.int32, (SLOTS, LANES), 0)
    low_half = lane < ROWS
    lane_all = lax.broadcasted_iota(jnp.int32, (LEVELS * SLOTS, LANES), 1)
    weight = jnp.zeros((SLOTS, LANES), F32)
    for b in range(SLOTS):
        flag = jnp.where(flags[pos * SLOTS + b] > 0, 1.0, 0.0)
        weight = jnp.where(slot == b, flag, weight)

    def send_strips(number):
        copies = []
        for side in range(2):
            copy = pltpu.make_async_remote_copy(
                src_ref=strips.at[number],
                dst_ref=arrived.at[1 - side, number],
                send_sem=strip_send.at[side, number],
                recv_sem=strip_recv.at[1 - side, number],
                device_id=ring[side],
                device_id_type=MESH,
            )
            copy.start()
            copies.append(copy)
        return copies

    strip_copies = []
    for number in range(4):
        loads[number].wait()

        def pack(t, acc, number=number):
            moved = pltpu.roll(q[number, :, tile(t + 1)], 2 * t, 1)
            return jnp.where((((lane_all + 1) & 63) >> 1) == t, moved, acc)

        packed = lax.fori_loop(0, PAIRS, pack, jnp.zeros((LEVELS * SLOTS, LANES), F32), unroll=4)
        strips[number, 0] = packed
        strips[number, 1] = jnp.where(
            lane_all < ROWS, q[number, :, tile(1)], q[number, :, tile(PAIRS)]
        )
        if number == 0:
            pl.semaphore_wait(barrier, len(partners))
        strip_copies.append(send_strips(number))

    loads[4].wait()
    loads[5].wait()

    def wide_strips(value, t, store):
        moved = pltpu.roll(value, (8 * t) % ROWS, 1)
        store[t // 8] = jnp.where((((lane + 4) & 63) >> 3) == t % 8, moved, store[t // 8])

    mstrips[...] = jnp.zeros_like(mstrips)

    def diagonal(t, _):
        centre = 6.0 + cc[:, tile(t)]
        inverse = weight / centre
        mi2[t] = inverse
        wide_strips(inverse, t, mstrips)
        mrow[2 * t] = jnp.where(low_half, centre, 0.0)
        mrow[2 * t + 1] = jnp.where(low_half, pltpu.roll(centre, 64, 1), 0.0)
        return 0

    lax.fori_loop(0, PAIRS, diagonal, 0, unroll=2)
    for place, t in enumerate((0, 1, PAIRS - 2, PAIRS - 1)):
        mstrips[4 + place] = mi2[t]

    def exchange(store, landing, send_sem, recv_sem):
        copies = []
        for side in range(2):
            copy = pltpu.make_async_remote_copy(
                src_ref=store,
                dst_ref=landing.at[1 - side],
                send_sem=send_sem.at[side],
                recv_sem=recv_sem.at[1 - side],
                device_id=ring[side],
                device_id_type=MESH,
            )
            copy.start()
            copies.append(copy)
        return copies

    m_copies = exchange(mstrips, marrived, m_send, m_recv)

    listed = own_lists[...]
    relative = (listed - (pos - 1) * SLOTS + total * SLOTS) % (total * SLOTS)
    chosen = []
    for direction in range(8):
        column = jnp.broadcast_to(relative[:, direction : direction + 1], (SLOTS, LANES))
        there = jnp.broadcast_to(listed[:, direction : direction + 1], (SLOTS, LANES)) >= 0
        which = column // SLOTS
        row = jnp.where(there, column % SLOTS, 0)
        chosen.append((row, [there & (which == side) for side in range(3)]))

    def take(direction, sources):
        row, sides = chosen[direction]
        result = jnp.zeros((SLOTS, LANES), F32)
        for source, side in zip(sources, sides):
            result = jnp.where(side, jnp.take_along_axis(source, row, axis=0), result)
        return result

    loads[6].wait()

    def factor(t, _):
        above = None
        for level in range(LEVELS):
            rows = pl.ds(level * SLOTS, SLOTS)
            pivot = 1.0
            if level > 0:
                lower = kk[pl.ds((level - 1) * SLOTS, SLOTS), tile(t)]
                pivot = pivot + lower
            if level < LEVELS - 1:
                upper = kk[rows, tile(t)]
                pivot = pivot + upper
            if level > 0:
                pivot = pivot - lower * above
            inverse = 1.0 / pivot
            ip[rows, tile(t)] = inverse
            if level > 0:
                gl[rows, tile(t)] = lower * inverse
            if level < LEVELS - 1:
                above = upper * inverse
                fu[rows, tile(t)] = above
        return 0

    lax.fori_loop(0, PAIRS, factor, 0)
    loads[7].wait()

    def fill_halos(number):
        for copy in strip_copies[number]:
            copy.wait()

        def fill(level, _):
            rows = pl.ds(pl.multiple_of(level * SLOTS, SLOTS), SLOTS)
            sides = [arrived[0, number, 0, rows], strips[number, 0, rows], arrived[1, number, 0, rows]]
            east = pltpu.roll(take(0, sides), 63, 1)
            west = pltpu.roll(take(1, sides), 65, 1)
            hx[number, rows] = jnp.where((lane & 1) == 1, east, west)
            ends = [arrived[0, number, 1, rows], strips[number, 1, rows], arrived[1, number, 1, rows]]
            end = jnp.where(low_half, take(2, ends), take(3, ends))
            q[number, rows, tile(0)] = end
            q[number, rows, tile(PAIRS + 1)] = end
            return 0

        lax.fori_loop(0, LEVELS, fill, 0)

    east_edge = (lane & 63) == 63
    west_edge = (lane & 63) == 0

    def advance(numbers, t):
        carried = {number: [] for number in numbers}
        for level in range(LEVELS):
            rows = pl.ds(level * SLOTS, SLOTS)
            zonal = q[2, rows, tile(t + 1)]
            meridional = q[3, rows, tile(t + 1)]
            from_west = zonal > 0.0
            from_south = meridional > 0.0
            speed_x = jnp.abs(zonal)
            speed_y = jnp.abs(meridional)
            stay = 1.0 - speed_x - speed_y
            inverse = ip[rows, tile(t)]
            for number in numbers:
                here = q[number, rows, tile(t + 1)]
                edge = pltpu.roll(hx[number, rows], (LANES - 2 * t) % LANES, 1)
                east = jnp.where(east_edge, edge, pltpu.roll(here, LANES - 1, 1))
                west = jnp.where(west_edge, edge, pltpu.roll(here, 1, 1))
                north = pltpu.roll(jnp.where(low_half, q[number, rows, tile(t + 2)], here), 64, 1)
                south = pltpu.roll(jnp.where(low_half, here, q[number, rows, tile(t)]), 64, 1)
                moved = (
                    stay * here
                    + speed_x * jnp.where(from_west, west, east)
                    + speed_y * jnp.where(from_south, south, north)
                )
                value = moved * inverse
                if level > 0:
                    value = value + gl[rows, tile(t)] * carried[number][-1]
                carried[number].append(value)
        solved = {}
        for number in numbers:
            values = carried[number]
            for level in range(LEVELS - 2, -1, -1):
                rows = pl.ds(level * SLOTS, SLOTS)
                values[level] = values[level] + fu[rows, tile(t)] * values[level + 1]
            for level in range(LEVELS):
                mixed[number, pl.ds(level * SLOTS, SLOTS), tile(t)] = values[level] * weight
            solved[number] = values
        return solved

    outs = (t_out, s_out, u_out, v_out)

    def write_out(number):
        copy = pltpu.make_async_copy(mixed.at[number], outs[number], out_sem.at[number])
        copy.start()
        return copy

    fill_halos(0)
    fill_halos(1)
    zstrips[...] = jnp.zeros_like(zstrips)

    def tracers(t, _):
        solved = advance((0, 1), t)
        gap = solved[0][0] - solved[1][0]
        for level in range(1, LEVELS):
            gap = gap + (solved[0][level] - solved[1][level])
        load = src[:, tile(t)] + gap * (1.0 / LEVELS)
        scaled = load * mi2[t]
        z2[t] = scaled
        wide_strips(scaled, t, zstrips)
        return 0

    lax.fori_loop(0, PAIRS, tracers, 0)
    for place, t in enumerate((0, 1, PAIRS - 2, PAIRS - 1)):
        zstrips[4 + place] = z2[t]
    z_copies = exchange(zstrips, zarrived, z_send, z_recv)
    out_copies = [write_out(0), write_out(1)]

    def share(phase, landing, mine, own, peers, send_sem, recv_sem):
        landing[own] = mine[...]
        copies = []
        for r, peer in enumerate(peers, 1):
            copy = pltpu.make_async_remote_copy(
                src_ref=mine,
                dst_ref=landing.at[own],
                send_sem=send_sem.at[phase, r],
                recv_sem=recv_sem.at[phase, own],
                device_id=peer,
                device_id_type=MESH,
            )
            copy.start()
            copies.append(copy)
        return copies

    def gather_sum(phase, copies, landing, mine, own, count, recv_sem):
        for r, copy in enumerate(copies, 1):
            copy.wait_send()
            sender = (own + count - r) % count
            pltpu.make_async_remote_copy(
                src_ref=mine,
                dst_ref=landing.at[sender],
                send_sem=recv_sem.at[phase, sender],
                recv_sem=recv_sem.at[phase, sender],
                device_id=ring[0],
                device_id_type=MESH,
            ).wait_recv()
        result = landing[0]
        for i in range(1, count):
            result = result + landing[i]
        return result

    def gathered(values):
        result = jnp.zeros((SLOTS, LANES), F32)
        for place, value in enumerate(values):
            result = jnp.where(slot == place, jnp.sum(value, axis=0, keepdims=True), result)
        return result

    zero = jnp.zeros((SLOTS, LANES), F32)

    def split(t, carry):
        last, line, norm, product = carry
        value = z2[t]
        for row, moved in ((2 * t, value), (2 * t + 1, pltpu.roll(value, 64, 1))):
            here = jnp.where(low_half, moved, 0.0)
            zx[row + HALO] = here
            ahead = pltpu.roll(here, LANES - 1, 1)
            wide = here + 0.5 * (ahead + pltpu.roll(here, 1, 1))
            norm = norm + here * here * mrow[row]
            product = product + (here * ahead + last * wide)
            last = here
        return last, line, norm, product

    _, _, norm, product = lax.fori_loop(0, PAIRS, split, (zero, zero, zero, zero), unroll=2)
    part[0] = gathered([norm, 2.0 * product])
    copies = share(0, near_a, part.at[0], low, near_peers, near_send, near_recv)

    fill_halos(2)
    fill_halos(3)

    def zonal_step(t, _):
        advance((2,), t)
        return 0

    lax.fori_loop(0, PAIRS, zonal_step, 0)
    out_copies.append(write_out(2))
    part[1] = gather_sum(0, copies, near_a, part.at[0], low, NEAR, near_recv)
    copies = share(0, far_a, part.at[1], far_id, far_peers, far_send, far_recv)

    def meridional_step(t, _):
        advance((3,), t)
        return 0

    lax.fori_loop(0, PAIRS, meridional_step, 0)
    out_copies.append(write_out(3))

    def widen(store, landing, halves, wide, interior):
        def sources(place):
            return [landing[0, place], store[place], landing[1, place]]

        for first, directions, places in (
            (0, (3, 6, 7), (6, 7)),
            (HALO + ROWS, (2, 4, 5), (4, 5)),
        ):
            for i, place in enumerate(places):
                line = take(directions[0], sources(place))
                corner = jnp.where(
                    (lane & 63) < 32,
                    take(directions[1], sources(place)),
                    take(directions[2], sources(place)),
                )
                wide[first + 2 * i] = jnp.where(low_half, line, pltpu.roll(corner, 64, 1))
                wide[first + 2 * i + 1] = jnp.where(low_half, pltpu.roll(line, 64, 1), corner)
        for group in range(4):
            halves[group] = jnp.where(
                (lane & 4) == 0, take(0, sources(group)), take(1, sources(group))
            )

        def rows(t, _):
            side = halves[t // 8]
            step = (8 * t) % ROWS
            even, odd = interior(t)
            wide[HALO + 2 * t] = jnp.where(low_half, even, pltpu.roll(side, 64 - step, 1))
            wide[HALO + 2 * t + 1] = jnp.where(
                low_half, odd, pltpu.roll(side, (LANES - step) % LANES, 1)
            )
            return 0

        lax.fori_loop(0, PAIRS, rows, 0, unroll=2)

    for copy in m_copies:
        copy.wait()
    widen(mstrips, marrived, vp.at[0], mx, lambda t: (mi2[t], pltpu.roll(mi2[t], 64, 1)))
    for copy in z_copies:
        copy.wait()
    widen(
        zstrips, zarrived, vp.at[0], zx,
        lambda t: (zx[HALO + 2 * t], zx[HALO + 2 * t + 1]),
    )

    both = gather_sum(0, copies, far_a, part.at[1], far_id, far_count, far_recv)
    both = jnp.sum(both, axis=1, keepdims=True)
    shift = jnp.broadcast_to(both[1:2] / both[0:1], (SLOTS, LANES))

    def neighbours(value):
        paired = pltpu.roll(value, 1, 1) + pltpu.roll(value, LANES - 1, 1)
        return paired, value + 0.5 * paired

    basis = [zx, vp.at[0], vp.at[1], vp.at[2], vp.at[3]]
    moments = []
    for power in range(4):
        old, new = basis[power], basis[power + 1]
        first, last = 1 + power, HALO + ROWS + 2 - power

        def advance_row(a, carry, old=old, new=new):
            here, paired, wide, behind = carry
            ahead = old[a + 1]
            ahead_paired, ahead_wide = neighbours(ahead)
            value = mx[a] * (paired + behind + ahead_wide) - shift * here
            new[a] = value
            return (ahead, ahead_paired, ahead_wide, wide), here, value

        behind = old[first - 1]
        here = old[first]
        carry = (here, *neighbours(here), neighbours(behind)[1])
        for a in range(first, HALO):
            carry, _, _ = advance_row(a, carry)

        def inner(r, state):
            carry, same, cross = state
            carry, here, value = advance_row(r + HALO, carry)
            centre = mrow[r]
            return carry, same + here * (centre * here), cross + here * (centre * value)

        carry, same, cross = lax.fori_loop(0, ROWS, inner, (carry, zero, zero), unroll=4)
        moments += [same, cross]
        for a in range(HALO + ROWS, last + 1):
            carry, _, _ = advance_row(a, carry)

    part[2] = gathered(moments)
    copies = share(1, near_b, part.at[2], low, near_peers, near_send, near_recv)
    part[3] = gather_sum(1, copies, near_b, part.at[2], low, NEAR, near_recv)
    copies = share(1, far_b, part.at[3], far_id, far_peers, far_send, far_recv)
    sums = gather_sum(1, copies, far_b, part.at[3], far_id, far_count, far_recv)
    sums = jnp.sum(sums, axis=1, keepdims=True)

    mu = [jnp.broadcast_to(sums[i : i + 1], (SLOTS, LANES)) for i in range(8)]
    rest = 1.0 - shift
    matrix = [[rest * mu[i + j] - mu[i + j + 1] for j in range(4)] for i in range(4)]
    lower = [[None] * 4 for _ in range(4)]
    pivots, inverses, ahead = [], [], []
    for j in range(4):
        pivot = matrix[j][j]
        for i in range(j):
            pivot = pivot - lower[j][i] * lower[j][i] * pivots[i]
        kept = pivot > 1e-6 * matrix[j][j]
        pivots.append(jnp.where(kept, pivot, 0.0) if j else pivot)
        inverses.append(jnp.where(kept, 1.0 / pivot, 0.0) if j else 1.0 / pivot)
        for i in range(j + 1, 4):
            entry = matrix[i][j]
            for m in range(j):
                entry = entry - lower[i][m] * lower[j][m] * pivots[m]
            lower[i][j] = entry * inverses[j]
        right = mu[j]
        for i in range(j):
            right = right - lower[j][i] * ahead[i]
        ahead.append(right)
    factors = [None] * 4
    for j in range(3, -1, -1):
        value = ahead[j] * inverses[j]
        for i in range(j + 1, 4):
            value = value - lower[i][j] * factors[i]
        factors[j] = value

    def level_row(a):
        value = factors[0] * basis[0][a]
        for j in range(1, 4):
            value = value + factors[j] * basis[j][a]
        return value

    def slopes(t, carry):
        behind, here = carry
        ahead = level_row(HALO + 2 * t + 1)
        beyond = level_row(HALO + 2 * t + 2)

        def zonal_slope(value):
            return 0.5 * (pltpu.roll(value, LANES - 1, 1) - pltpu.roll(value, 1, 1))

        def joined(even, odd):
            return jnp.where(low_half, even, pltpu.roll(odd, 64, 1))

        sx_out[:, tile(t)] = joined(zonal_slope(here), zonal_slope(ahead))
        sy_out[:, tile(t)] = joined(0.5 * (ahead - behind), 0.5 * (beyond - here))
        h_out[:, tile(t)] = joined(here, ahead)
        return ahead, beyond

    lax.fori_loop(0, PAIRS, slopes, (level_row(HALO - 1), level_row(HALO)), unroll=2)
    for copy in out_copies:
        copy.wait()


def finish_kernel(t_in, s_in, u_in, v_in, sx, sy, h, t_out, s_out, u_out, v_out, h_out):
    t_out[...] = t_in[...]
    s_out[...] = s_in[...]
    h_out[...] = h[...]
    for level in range(LEVELS):
        rows = pl.ds(level * SLOTS, SLOTS)
        u_out[rows] = u_in[rows] - sx[...]
        v_out[rows] = v_in[rows] - sy[...]


def finish(fields, extras, chunks=4):
    width = CELLS // chunks
    wide = pl.BlockSpec((LEVELS * SLOTS, width), lambda i: (0, i))
    thin = pl.BlockSpec((SLOTS, width), lambda i: (0, i))
    big = jax.ShapeDtypeStruct((LEVELS * SLOTS, CELLS), F32)
    small = jax.ShapeDtypeStruct((SLOTS, CELLS), F32)
    return pl.pallas_call(
        finish_kernel,
        grid=(chunks,),
        in_specs=[wide] * 4 + [thin] * 3,
        out_specs=[wide] * 4 + [thin],
        out_shape=[big] * 4 + [small],
        name="finish",
    )(*fields, *extras)


def local(sizes, t, s, u, v, k, c, g, flags, lists):
    stacked = LEVELS * SLOTS
    fields = [x.reshape(stacked, CELLS) for x in (t, s, u, v)]
    big = jax.ShapeDtypeStruct((stacked, CELLS), F32)
    small = jax.ShapeDtypeStruct((SLOTS, CELLS), F32)
    anywhere = pl.BlockSpec(memory_space=pl.ANY)
    vmem = pl.BlockSpec(memory_space=pltpu.VMEM)
    dma = pltpu.SemaphoreType.DMA
    far_count = sizes[0] * sizes[1] // NEAR
    tall = ROWS + 2 * HALO
    results = pl.pallas_call(
        functools.partial(kernel, sizes),
        out_shape=[big] * 4 + [small] * 3,
        in_specs=[anywhere] * 7 + [pl.BlockSpec(memory_space=pltpu.SMEM), anywhere],
        out_specs=[anywhere] * 4 + [vmem] * 3,
        scratch_shapes=[
            pltpu.VMEM((4, stacked, CELLS + 2 * LANES), F32),
            pltpu.VMEM((stacked - SLOTS, CELLS), F32),
            pltpu.VMEM((SLOTS, CELLS), F32),
            pltpu.VMEM((SLOTS, CELLS), F32),
            pltpu.VMEM((SLOTS, 8), jnp.int32),
            pltpu.VMEM((4, stacked, CELLS), F32),
            pltpu.VMEM((stacked, CELLS), F32),
            pltpu.VMEM((stacked, CELLS), F32),
            pltpu.VMEM((stacked, CELLS), F32),
            pltpu.VMEM((4, stacked, LANES), F32),
            pltpu.VMEM((4, 2, stacked, LANES), F32),
            pltpu.VMEM((2, 4, 2, stacked, LANES), F32),
            pltpu.VMEM((8, SLOTS, LANES), F32),
            pltpu.VMEM((2, 8, SLOTS, LANES), F32),
            pltpu.VMEM((8, SLOTS, LANES), F32),
            pltpu.VMEM((2, 8, SLOTS, LANES), F32),
            pltpu.VMEM((PAIRS, SLOTS, LANES), F32),
            pltpu.VMEM((PAIRS, SLOTS, LANES), F32),
            pltpu.VMEM((tall, SLOTS, LANES), F32),
            pltpu.VMEM((tall, SLOTS, LANES), F32),
            pltpu.VMEM((ROWS, SLOTS, LANES), F32),
            pltpu.VMEM((4, tall, SLOTS, LANES), F32),
            pltpu.VMEM((4, SLOTS, LANES), F32),
            pltpu.VMEM((NEAR, SLOTS, LANES), F32),
            pltpu.VMEM((far_count, SLOTS, LANES), F32),
            pltpu.VMEM((NEAR, SLOTS, LANES), F32),
            pltpu.VMEM((far_count, SLOTS, LANES), F32),
            dma((8,)),
            dma((4,)),
            dma((2, 4)),
            dma((2, 4)),
            dma((2,)),
            dma((2,)),
            dma((2,)),
            dma((2,)),
            dma((2, NEAR)),
            dma((2, NEAR)),
            dma((2, far_count)),
            dma((2, far_count)),
        ],
        compiler_params=pltpu.CompilerParams(
            collective_id=0, has_side_effects=True, vmem_limit_bytes=40 * 1024 * 1024
        ),
        name="ocean_step",
    )(*fields, k.reshape(stacked - SLOTS, CELLS), c, g, flags, lists)
    done = finish(results[:4], results[4:])
    shape = (LEVELS, SLOTS, CELLS)
    return tuple(x.reshape(shape) for x in done[:4]) + (done[4],)


def solution(mesh):
    whole = P(None, ("gx", "gy"), None)
    flat = P(("gx", "gy"), None)
    return jax.shard_map(
        functools.partial(local, (mesh.shape["gx"], mesh.shape["gy"])),
        mesh=mesh,
        in_specs=(whole, whole, whole, whole, whole, flat, flat, P(), P()),
        out_specs=(whole, whole, whole, whole, flat),
        check_vma=False,
    )
```

time: 837 us -> 76 us (0.09); the launches traced: 826 us -> 75.5 us
  blocking collectives: 441 us -> 0 us
  local copies, waits for them, and re-layouts: 240 us -> 13 us
  starting transfers between devices: 66.4 us -> 0 us
  other arithmetic: 62.6 us -> 0 us
  Pallas kernels: 0 us -> 61.8 us
  between operations: 12.8 us -> 0.72 us
    psum x7 -> x0, blocking collectives: 441 us -> none  [the longest x4 253 us: squared_norm(): return lax.psum(jnp.sum(residual * scaled), ('gx', 'gy'))]
    ppermute x24 -> x0, starting transfers between devices: 66.4 us -> none  [the longest x22 66.2 us: passed_along(): return lax.ppermute(value, axis, pairs)]
    pallas_call x0 -> x2, Pallas kernels: none -> 61.8 us  [the longest x1 57 us: local(): pl.pallas_call(functools.partial(kernel, sizes), out_shape=[big] * 4 + [s...]
    another operation x82 -> x0, local copies, waits for them, and re-layouts: 51.2 us -> none  [the longest x74 49.2 us: across(): return jnp.tile(border, (1,) * (border.ndim - 1) + (BSIDE,))]
    slice x48 -> x0, local copies, waits for them, and re-layouts: 43.5 us -> none  [the longest x6 18.1 us: edge_strips(): square[..., :, -1]]
    gather x45 -> x0, local copies, waits for them, and re-layouts: 36.1 us -> none  [the longest x40 31.9 us: picked(): jnp.take(strips, source[:, column], axis=-2)[..., start:start + length]]
    reshape x28 -> x0, local copies, waits for them, and re-layouts: 35.2 us -> none  [the longest x24 29.3 us: along_rows(): return jnp.repeat(border, BSIDE, axis=-1)]
    squeeze x32 -> x0, local copies, waits for them, and re-layouts: 23.2 us -> none  [the longest x4 9.22 us: edge_strips(): square[..., :, 0]]
  transfers between devices with their start and end apart: 24 -> 0, of which waited for: 2 -> 0; matrix products, arithmetic and copies ran while one was open for 7% -> 0% of each run, Pallas kernels for 0% -> 0%
where the time goes in v1:
time: 76 us; the launch traced here: 75.5 us
  Pallas kernels  61.8 us (81%)
  local copies, waits for them, and re-layouts  13 us (17%)
    pallas_call x1, Pallas kernels, local(): pl.pallas_call(functools.partial(kernel, sizes), out_shape=[big] * 4 + [s...  57 us
    unnamed x31, local copies, waits for them, and re-layouts  13 us
    pallas_call x1, Pallas kernels, finish(): pl.pallas_call(finish_kernel, grid=(chunks,), in_specs=[wide] * 4 + [thin...  4.76 us

profile of v1, /device:TPU:0, one launch (start us, length us, event | category | flops | bytes accessed | tf_op | source)
XLA Modules:
  0.0 75.5 jit_solution(8335361970625867704)
XLA Ops:
  0.6 0.0 copy-start.9
  0.6 0.0 copy-start.10
  0.7 0.0 copy-start.14
  0.7 1.0 %copy.14.lists = s32[1024,8]{1,0:T(8,128)S(1)} copy(s32[1024,8]{0,1:T(8,128)} %param.17) | data formatting | bytes 65536 | tf_op args[8]
  1.7 0.0 copy-done.9
  1.7 0.0 copy-done.10
  1.7 0.0 copy-done.14
  1.7 0.0 copy-start
  1.7 1.2 %copy-done = f32[8,8,4096]{2,1,0:T(8,128)S(1)} copy-done((f32[8,8,4096]{2,1,0:T(8,128)S(1)}, f32[8,8,4096]{2,1,0:T(8,128)}, u32[]{:S(2)}) %copy-start) | copy-done | bytes 1048600
  2.9 0.0 copy-start.1
  2.9 1.2 %copy-done.1 = f32[8,8,4096]{2,1,0:T(8,128)S(1)} copy-done((f32[8,8,4096]{2,1,0:T(8,128)S(1)}, f32[8,8,4096]{2,1,0:T(8,128)}, u32[]{:S(2)}) %copy-start.1) | copy-done | bytes 1048600
  4.1 0.0 copy-start.2
  4.1 1.2 %copy-done.2 = f32[8,8,4096]{2,1,0:T(8,128)S(1)} copy-done((f32[8,8,4096]{2,1,0:T(8,128)S(1)}, f32[8,8,4096]{2,1,0:T(8,128)}, u32[]{:S(2)}) %copy-start.2) | copy-done | bytes 1048600
  5.4 0.0 copy-start.3
  5.4 1.2 %copy-done.3 = f32[8,8,4096]{2,1,0:T(8,128)S(1)} copy-done((f32[8,8,4096]{2,1,0:T(8,128)S(1)}, f32[8,8,4096]{2,1,0:T(8,128)}, u32[]{:S(2)}) %copy-start.3) | copy-done | bytes 1048600
  6.6 0.0 copy-start.8
  6.6 1.2 %copy-done.8 = f32[7,8,4096]{2,1,0:T(8,128)S(1)} copy-done((f32[7,8,4096]{2,1,0:T(8,128)S(1)}, f32[7,8,4096]{2,1,0:T(8,128)}, u32[]{:S(2)}) %copy-start.8) | copy-done | bytes 917528
  7.8 57.0 %ocean_step.1 = (f32[64,4096]{1,0:T(8,128)S(1)}, f32[64,4096]{1,0:T(8,128)S(1)}, f32[64,4096]{1,0:T(8,128)S(1)}, f32[64,4096]{1,0:T(8,128)S(1)}, f32[8,4096]{1,0...) custom-call(f32[64,4096]{1,0:T(8,128)S(1)} %bitcast.9, f32[64,4096]{1,0:T(8,128)S(1)} %bitcast.10, ...), custom_call_target="tpu_custom_call" | custom-call | tf_op jit(solution)/shard_map/ocean_step/pallas_call | solution.py:539
  64.8 0.0 copy-start.4
  64.8 1.0 %copy-done.4 = f32[64,4096]{1,0:T(8,128)} copy-done((f32[64,4096]{1,0:T(8,128)}, f32[64,4096]{1,0:T(8,128)S(1)}, u32[]{:S(2)}) %copy-start.4) | copy-done | bytes 1048600
  65.8 0.0 copy-start.5
  65.8 1.0 %copy-done.5 = f32[64,4096]{1,0:T(8,128)} copy-done((f32[64,4096]{1,0:T(8,128)}, f32[64,4096]{1,0:T(8,128)S(1)}, u32[]{:S(2)}) %copy-start.5) | copy-done | bytes 1048600
  66.8 0.0 copy-start.6
  66.8 1.0 %copy-done.6 = f32[64,4096]{1,0:T(8,128)} copy-done((f32[64,4096]{1,0:T(8,128)}, f32[64,4096]{1,0:T(8,128)S(1)}, u32[]{:S(2)}) %copy-start.6) | copy-done | bytes 1048600
  67.7 0.0 copy-start.7
  67.7 1.0 %copy-done.7 = f32[64,4096]{1,0:T(8,128)} copy-done((f32[64,4096]{1,0:T(8,128)}, f32[64,4096]{1,0:T(8,128)S(1)}, u32[]{:S(2)}) %copy-start.7) | copy-done | bytes 1048600
  68.7 0.0 copy-start.11
  68.7 0.7 copy-done.11
  69.4 0.0 copy-start.12
  69.4 0.7 copy-done.12
  70.1 0.7 copy-done.13
  70.7 4.8 %finish.1 = (f32[64,4096]{1,0:T(8,128)}, f32[64,4096]{1,0:T(8,128)}, f32[64,4096]{1,0:T(8,128)}, f32[64,4096]{1,0:T(8,128)}, f32[8,4096]{1,0:T(8,128)}) custom-call(f32[64,4096]{1,0:T(8,128)} %copy-done.4, f32[64,4096]{1,0:T(8,128)} %copy-done.5, f32[64,4096]{1,0:T(8,128)} %copy-done.6, f32[64,4096]{1,0:T(8,128)} %copy-done.7, f32[8,4096]{1,0:T(8,128)} %copy-done.11, ...), custom_call_target="tpu_custom_call" | custom-call | tf_op jit(solution)/shard_map/finish/pallas_call | solution.py:519
  (1 shorter events, 0.0 us)
Async XLA Ops:
  0.6 1.0 %copy-start.9 = (f32[8,4096]{1,0:T(8,128)S(1)}, f32[8,4096]{1,0:T(8,128)}, u32[]{:S(2)}) copy-start(f32[8,4096]{1,0:T(8,128)} %c_in.1) | copy-start | bytes 393220
  0.6 1.0 %copy-start.10 = (f32[8,4096]{1,0:T(8,128)S(1)}, f32[8,4096]{1,0:T(8,128)}, u32[]{:S(2)}) copy-start(f32[8,4096]{1,0:T(8,128)} %g_in.1) | copy-start | bytes 393220
  0.7 1.0 %copy-start.14 = (s32[1024]{0:T(1024)S(1)}, s32[1024]{0:T(1024)}, u32[]{:S(2)}) copy-start(s32[1024]{0:T(1024)} %flags.1) | copy-start | bytes 12292
  1.7 1.2 %copy-start = (f32[8,8,4096]{2,1,0:T(8,128)S(1)}, f32[8,8,4096]{2,1,0:T(8,128)}, u32[]{:S(2)}) copy-start(f32[8,8,4096]{2,1,0:T(8,128)} %param.9) | copy-start | bytes 3145732
  2.9 1.2 %copy-start.1 = (f32[8,8,4096]{2,1,0:T(8,128)S(1)}, f32[8,8,4096]{2,1,0:T(8,128)}, u32[]{:S(2)}) copy-start(f32[8,8,4096]{2,1,0:T(8,128)} %param.10) | copy-start | bytes 3145732
  4.1 1.2 %copy-start.2 = (f32[8,8,4096]{2,1,0:T(8,128)S(1)}, f32[8,8,4096]{2,1,0:T(8,128)}, u32[]{:S(2)}) copy-start(f32[8,8,4096]{2,1,0:T(8,128)} %param.11) | copy-start | bytes 3145732
  5.4 1.2 %copy-start.3 = (f32[8,8,4096]{2,1,0:T(8,128)S(1)}, f32[8,8,4096]{2,1,0:T(8,128)}, u32[]{:S(2)}) copy-start(f32[8,8,4096]{2,1,0:T(8,128)} %param.12) | copy-start | bytes 3145732
  6.6 1.2 %copy-start.8 = (f32[7,8,4096]{2,1,0:T(8,128)S(1)}, f32[7,8,4096]{2,1,0:T(8,128)}, u32[]{:S(2)}) copy-start(f32[7,8,4096]{2,1,0:T(8,128)} %param.13) | copy-start | bytes 2752516
  64.8 1.0 %copy-start.4 = (f32[64,4096]{1,0:T(8,128)}, f32[64,4096]{1,0:T(8,128)S(1)}, u32[]{:S(2)}) copy-start(f32[64,4096]{1,0:T(8,128)S(1)} %get-tuple-element.17.t_in) | copy-start | bytes 3145732
  65.8 1.0 %copy-start.5 = (f32[64,4096]{1,0:T(8,128)}, f32[64,4096]{1,0:T(8,128)S(1)}, u32[]{:S(2)}) copy-start(f32[64,4096]{1,0:T(8,128)S(1)} %get-tuple-element.18.s_in) | copy-start | bytes 3145732
  66.8 1.0 %copy-start.6 = (f32[64,4096]{1,0:T(8,128)}, f32[64,4096]{1,0:T(8,128)S(1)}, u32[]{:S(2)}) copy-start(f32[64,4096]{1,0:T(8,128)S(1)} %get-tuple-element.19.u_in) | copy-start | bytes 3145732
  67.7 1.0 %copy-start.7 = (f32[64,4096]{1,0:T(8,128)}, f32[64,4096]{1,0:T(8,128)S(1)}, u32[]{:S(2)}) copy-start(f32[64,4096]{1,0:T(8,128)S(1)} %get-tuple-element.20.v_in) | copy-start | bytes 3145732
  68.7 0.7 copy-start.11
  69.4 0.7 copy-start.12
  70.1 0.7 copy-start.13

commit v2 on v1

--- a/solution.py
+++ b/solution.py
@@ -9,6 +9,7 @@
 
 MESH = pl.DeviceIdType.MESH
 F32 = jnp.float32
+BF16 = jnp.bfloat16
 LANES = 128
 SLOTS = 8
 LEVELS = 8
@@ -16,6 +17,7 @@
 CELLS = 4096
 ROWS = 64
 HALO = 4
+CHUNK = 8
 NEAR = 8
 
 
@@ -25,11 +27,12 @@
 
 def kernel(
     sizes,
-    t_in, s_in, u_in, v_in, k_in, c_in, g_in, flags, lists,
+    t_in, s_in, u_in, v_in, k_in, c_in, g_in, flags_in, lists,
     t_out, s_out, u_out, v_out, sx_out, sy_out, h_out,
-    q, kk, cc, src, own_lists, mixed, ip, fu, gl, hx,
+    q, kk, cc, src, own_lists, flags, mixed, ip, fu, gl, hx,
+    east_of, west_of, half_of, edge_of, shifts, spread,
     strips, arrived, mstrips, marrived, zstrips, zarrived,
-    z2, mi2, zx, mx, mrow, vp, part, near_a, far_a, near_b, far_b,
+    z2, mi2, zx, mx, mrow, v1, v2, v3, v4, part, near_a, far_a, near_b, far_b,
     in_sem, out_sem, strip_send, strip_recv, m_send, m_recv, z_send, z_recv,
     near_send, near_recv, far_send, far_recv,
 ):
@@ -57,23 +60,23 @@
     loads = []
     for number, ref in enumerate((t_in, s_in, u_in, v_in)):
         loads.append(
-            pltpu.make_async_copy(ref, q.at[number, :, pl.ds(LANES, CELLS)], in_sem.at[number])
+            pltpu.make_async_copy(ref, q.at[number], in_sem.at[number])
         )
-    loads.append(pltpu.make_async_copy(lists.at[pl.ds(pos * SLOTS, SLOTS)], own_lists, in_sem.at[4]))
+    loads.append(pltpu.make_async_copy(
+            lists.at[:, tile(pos // (LANES // SLOTS))], own_lists, in_sem.at[4]
+        ))
     loads.append(pltpu.make_async_copy(c_in, cc, in_sem.at[5]))
     loads.append(pltpu.make_async_copy(k_in, kk, in_sem.at[6]))
     loads.append(pltpu.make_async_copy(g_in, src, in_sem.at[7]))
     for load in loads:
         load.start()
+    flag_load = pltpu.make_async_copy(flags_in, flags, in_sem.at[8])
+    flag_load.start()
 
     lane = lax.broadcasted_iota(jnp.int32, (SLOTS, LANES), 1)
     slot = lax.broadcasted_iota(jnp.int32, (SLOTS, LANES), 0)
     low_half = lane < ROWS
     lane_all = lax.broadcasted_iota(jnp.int32, (LEVELS * SLOTS, LANES), 1)
-    weight = jnp.zeros((SLOTS, LANES), F32)
-    for b in range(SLOTS):
-        flag = jnp.where(flags[pos * SLOTS + b] > 0, 1.0, 0.0)
-        weight = jnp.where(slot == b, flag, weight)
 
     def send_strips(number):
         copies = []
@@ -90,44 +93,94 @@
             copies.append(copy)
         return copies
 
+    row = lax.broadcasted_iota(jnp.int32, (2 * LANES, LANES), 0) % LANES
+    column = lax.broadcasted_iota(jnp.int32, (2 * LANES, LANES), 1)
+    odd = column % 2 == 1
+    upper_odd = (column >= 63) & (column < 127)
+    packing = jnp.where(
+        odd, jnp.where(upper_odd, 63, 127), jnp.where(column < ROWS, 0, ROWS)
+    )
+    edge_row = row % 2 == 1
+    target = jnp.where(
+        edge_row,
+        jnp.where((row >= 63) & (row < 127), 0, ROWS),
+        jnp.where(row < ROWS, 63, 127),
+    )
+    for place, chosen_lanes in enumerate(
+        (
+            (row == column + 1) & (column % ROWS != ROWS - 1),
+            (row == column - 1) & (column % ROWS != 0),
+            row == (column + ROWS) % LANES,
+            row == packing,
+        )
+    ):
+        shifts[:, place * LANES : (place + 1) * LANES] = jnp.where(chosen_lanes, 1.0, 0.0).astype(BF16)
+    spread[...] = jnp.where(column == target, 1.0, 0.0).astype(BF16)
+
+    def parts(value):
+        high = value.astype(BF16)
+        rest = (value - high.astype(F32)).astype(BF16)
+        return jnp.concatenate([high, rest], axis=1)
+
+    stacked = LEVELS * SLOTS
     strip_copies = []
     for number in range(4):
         loads[number].wait()
 
-        def pack(t, acc, number=number):
-            moved = pltpu.roll(q[number, :, tile(t + 1)], 2 * t, 1)
-            return jnp.where((((lane_all + 1) & 63) >> 1) == t, moved, acc)
-
-        packed = lax.fori_loop(0, PAIRS, pack, jnp.zeros((LEVELS * SLOTS, LANES), F32), unroll=4)
-        strips[number, 0] = packed
+        def shift_all(chunk, acc, number=number):
+            first = chunk * CHUNK
+            split_parts = jnp.concatenate(
+                [parts(q[number, :, tile(first + i)]) for i in range(CHUNK)], axis=0
+            )
+            moved = jnp.dot(split_parts, shifts[...], preferred_element_type=F32)
+            for i in range(CHUNK):
+                rows = slice(i * stacked, (i + 1) * stacked)
+                east_of[number, :, tile(first + i)] = moved[rows, :LANES]
+                west_of[number, :, tile(first + i)] = moved[rows, LANES : 2 * LANES]
+                half_of[number, :, tile(first + i + 1)] = moved[rows, 2 * LANES : 3 * LANES]
+                here = (((lane_all + 1) & 63) >> 1) == first + i
+                acc = jnp.where(here, moved[rows, 3 * LANES :], acc)
+            return acc
+
+        strips[number, 0] = lax.fori_loop(
+            0, PAIRS // CHUNK, shift_all, jnp.zeros((stacked, LANES), F32)
+        )
         strips[number, 1] = jnp.where(
-            lane_all < ROWS, q[number, :, tile(1)], q[number, :, tile(PAIRS)]
+            lane_all < ROWS, q[number, :, tile(0)], q[number, :, tile(PAIRS - 1)]
         )
         if number == 0:
             pl.semaphore_wait(barrier, len(partners))
         strip_copies.append(send_strips(number))
 
+    flag_load.wait()
+    weight = jnp.zeros((SLOTS, LANES), F32)
+    for b in range(SLOTS):
+        flag = jnp.where(flags[pos * SLOTS + b] > 0, 1.0, 0.0)
+        weight = jnp.where(slot == b, flag, weight)
+
     loads[4].wait()
     loads[5].wait()
 
-    def wide_strips(value, t, store):
-        moved = pltpu.roll(value, (8 * t) % ROWS, 1)
-        store[t // 8] = jnp.where((((lane + 4) & 63) >> 3) == t % 8, moved, store[t // 8])
-
-    mstrips[...] = jnp.zeros_like(mstrips)
+    def wide_strips(value_of, store):
+        for group in range(4):
+            packed = jnp.zeros((SLOTS, LANES), F32)
+            for k in range(8):
+                value = value_of[8 * group + k]
+                moved = pltpu.roll(value, 8 * k, 1) if k else value
+                packed = jnp.where((((lane + 4) & 63) >> 3) == k, moved, packed)
+            store[group] = packed
+        for place, t in enumerate((0, 1, PAIRS - 2, PAIRS - 1)):
+            store[4 + place] = value_of[t]
 
     def diagonal(t, _):
         centre = 6.0 + cc[:, tile(t)]
-        inverse = weight / centre
-        mi2[t] = inverse
-        wide_strips(inverse, t, mstrips)
+        mi2[t] = weight / centre
         mrow[2 * t] = jnp.where(low_half, centre, 0.0)
         mrow[2 * t + 1] = jnp.where(low_half, pltpu.roll(centre, 64, 1), 0.0)
         return 0
 
-    lax.fori_loop(0, PAIRS, diagonal, 0, unroll=2)
-    for place, t in enumerate((0, 1, PAIRS - 2, PAIRS - 1)):
-        mstrips[4 + place] = mi2[t]
+    lax.fori_loop(0, PAIRS, diagonal, 0, unroll=8)
+    wide_strips(mi2, mstrips)
 
     def exchange(store, landing, send_sem, recv_sem):
         copies = []
@@ -146,12 +199,16 @@
 
     m_copies = exchange(mstrips, marrived, m_send, m_recv)
 
-    listed = own_lists[...]
-    relative = (listed - (pos - 1) * SLOTS + total * SLOTS) % (total * SLOTS)
+    listed_lanes = pltpu.roll(
+        own_lists[...].astype(F32), (LANES - (pos % (LANES // SLOTS)) * SLOTS) % LANES, 1
+    )
     chosen = []
     for direction in range(8):
-        column = jnp.broadcast_to(relative[:, direction : direction + 1], (SLOTS, LANES))
-        there = jnp.broadcast_to(listed[:, direction : direction + 1], (SLOTS, LANES)) >= 0
+        line = jnp.broadcast_to(listed_lanes[direction : direction + 1], (SLOTS, LANES))
+        own = jnp.sum(jnp.where(lane == slot, line, 0.0), axis=1, keepdims=True)
+        listed = jnp.broadcast_to(own, (SLOTS, LANES)).astype(jnp.int32)
+        column = (listed - (pos - 1) * SLOTS + total * SLOTS) % (total * SLOTS)
+        there = listed >= 0
         which = column // SLOTS
         row = jnp.where(there, column % SLOTS, 0)
         chosen.append((row, [there & (which == side) for side in range(3)]))
@@ -179,7 +236,7 @@
             if level > 0:
                 pivot = pivot - lower * above
             inverse = 1.0 / pivot
-            ip[rows, tile(t)] = inverse
+            ip[rows, tile(t)] = inverse * weight
             if level > 0:
                 gl[rows, tile(t)] = lower * inverse
             if level < LEVELS - 1:
@@ -187,26 +244,38 @@
                 fu[rows, tile(t)] = above
         return 0
 
-    lax.fori_loop(0, PAIRS, factor, 0)
+    lax.fori_loop(0, PAIRS, factor, 0, unroll=2)
     loads[7].wait()
 
     def fill_halos(number):
         for copy in strip_copies[number]:
             copy.wait()
 
-        def fill(level, _):
-            rows = pl.ds(pl.multiple_of(level * SLOTS, SLOTS), SLOTS)
+        for level in range(LEVELS):
+            rows = pl.ds(level * SLOTS, SLOTS)
             sides = [arrived[0, number, 0, rows], strips[number, 0, rows], arrived[1, number, 0, rows]]
-            east = pltpu.roll(take(0, sides), 63, 1)
-            west = pltpu.roll(take(1, sides), 65, 1)
-            hx[number, rows] = jnp.where((lane & 1) == 1, east, west)
+            hx[number, rows] = jnp.where((lane & 1) == 1, take(1, sides), take(0, sides))
             ends = [arrived[0, number, 1, rows], strips[number, 1, rows], arrived[1, number, 1, rows]]
-            end = jnp.where(low_half, take(2, ends), take(3, ends))
-            q[number, rows, tile(0)] = end
-            q[number, rows, tile(PAIRS + 1)] = end
+            end = pltpu.roll(jnp.where(low_half, take(2, ends), take(3, ends)), 64, 1)
+            half_of[number, rows, tile(0)] = end
+            half_of[number, rows, tile(PAIRS + 1)] = end
+        halo_parts = parts(hx[number])
+
+        def edges(chunk, _):
+            first = chunk * CHUNK
+            position = lax.broadcasted_iota(jnp.int32, (stacked, 2 * LANES), 1)
+            pieces = []
+            for i in range(CHUNK):
+                here = (((position + 1) & 63) >> 1) == first + i
+                pieces.append(jnp.where(here, halo_parts, jnp.zeros_like(halo_parts)))
+            found = jnp.dot(
+                jnp.concatenate(pieces, axis=0), spread[...], preferred_element_type=F32
+            )
+            for i in range(CHUNK):
+                edge_of[number, :, tile(first + i)] = found[i * stacked : (i + 1) * stacked]
             return 0
 
-        lax.fori_loop(0, LEVELS, fill, 0)
+        lax.fori_loop(0, PAIRS // CHUNK, edges, 0)
 
     east_edge = (lane & 63) == 63
     west_edge = (lane & 63) == 0
@@ -215,26 +284,23 @@
         carried = {number: [] for number in numbers}
         for level in range(LEVELS):
             rows = pl.ds(level * SLOTS, SLOTS)
-            zonal = q[2, rows, tile(t + 1)]
-            meridional = q[3, rows, tile(t + 1)]
+            zonal = q[2, rows, tile(t)]
+            meridional = q[3, rows, tile(t)]
             from_west = zonal > 0.0
             from_south = meridional > 0.0
+            outside = (east_edge & jnp.logical_not(from_west)) | (west_edge & from_west)
+            behind = low_half & from_south
+            beyond = jnp.logical_not(low_half | from_south)
             speed_x = jnp.abs(zonal)
             speed_y = jnp.abs(meridional)
             stay = 1.0 - speed_x - speed_y
             inverse = ip[rows, tile(t)]
             for number in numbers:
-                here = q[number, rows, tile(t + 1)]
-                edge = pltpu.roll(hx[number, rows], (LANES - 2 * t) % LANES, 1)
-                east = jnp.where(east_edge, edge, pltpu.roll(here, LANES - 1, 1))
-                west = jnp.where(west_edge, edge, pltpu.roll(here, 1, 1))
-                north = pltpu.roll(jnp.where(low_half, q[number, rows, tile(t + 2)], here), 64, 1)
-                south = pltpu.roll(jnp.where(low_half, here, q[number, rows, tile(t)]), 64, 1)
-                moved = (
-                    stay * here
-                    + speed_x * jnp.where(from_west, west, east)
-                    + speed_y * jnp.where(from_south, south, north)
-                )
+                along = jnp.where(from_west, west_of[number, rows, tile(t)], east_of[number, rows, tile(t)])
+                along = jnp.where(outside, edge_of[number, rows, tile(t)], along)
+                across = jnp.where(beyond, half_of[number, rows, tile(t + 2)], half_of[number, rows, tile(t + 1)])
+                across = jnp.where(behind, half_of[number, rows, tile(t)], across)
+                moved = stay * q[number, rows, tile(t)] + speed_x * along + speed_y * across
                 value = moved * inverse
                 if level > 0:
                     value = value + gl[rows, tile(t)] * carried[number][-1]
@@ -246,7 +312,7 @@
                 rows = pl.ds(level * SLOTS, SLOTS)
                 values[level] = values[level] + fu[rows, tile(t)] * values[level + 1]
             for level in range(LEVELS):
-                mixed[number, pl.ds(level * SLOTS, SLOTS), tile(t)] = values[level] * weight
+                mixed[number, pl.ds(level * SLOTS, SLOTS), tile(t)] = values[level]
             solved[number] = values
         return solved
 
@@ -259,7 +325,6 @@
 
     fill_halos(0)
     fill_halos(1)
-    zstrips[...] = jnp.zeros_like(zstrips)
 
     def tracers(t, _):
         solved = advance((0, 1), t)
@@ -269,12 +334,10 @@
         load = src[:, tile(t)] + gap * (1.0 / LEVELS)
         scaled = load * mi2[t]
         z2[t] = scaled
-        wide_strips(scaled, t, zstrips)
         return 0
 
     lax.fori_loop(0, PAIRS, tracers, 0)
-    for place, t in enumerate((0, 1, PAIRS - 2, PAIRS - 1)):
-        zstrips[4 + place] = z2[t]
+    wide_strips(z2, zstrips)
     z_copies = exchange(zstrips, zarrived, z_send, z_recv)
     out_copies = [write_out(0), write_out(1)]
 
@@ -332,7 +395,7 @@
             last = here
         return last, line, norm, product
 
-    _, _, norm, product = lax.fori_loop(0, PAIRS, split, (zero, zero, zero, zero), unroll=2)
+    _, _, norm, product = lax.fori_loop(0, PAIRS, split, (zero, zero, zero, zero), unroll=8)
     part[0] = gathered([norm, 2.0 * product])
     copies = share(0, near_a, part.at[0], low, near_peers, near_send, near_recv)
 
@@ -387,15 +450,15 @@
             )
             return 0
 
-        lax.fori_loop(0, PAIRS, rows, 0, unroll=2)
+        lax.fori_loop(0, PAIRS, rows, 0, unroll=8)
 
     for copy in m_copies:
         copy.wait()
-    widen(mstrips, marrived, vp.at[0], mx, lambda t: (mi2[t], pltpu.roll(mi2[t], 64, 1)))
+    widen(mstrips, marrived, v1, mx, lambda t: (mi2[t], pltpu.roll(mi2[t], 64, 1)))
     for copy in z_copies:
         copy.wait()
     widen(
-        zstrips, zarrived, vp.at[0], zx,
+        zstrips, zarrived, v1, zx,
         lambda t: (zx[HALO + 2 * t], zx[HALO + 2 * t + 1]),
     )
 
@@ -407,7 +470,7 @@
         paired = pltpu.roll(value, 1, 1) + pltpu.roll(value, LANES - 1, 1)
         return paired, value + 0.5 * paired
 
-    basis = [zx, vp.at[0], vp.at[1], vp.at[2], vp.at[3]]
+    basis = [zx, v1, v2, v3, v4]
     moments = []
     for power in range(4):
         old, new = basis[power], basis[power + 1]
@@ -433,7 +496,7 @@
             centre = mrow[r]
             return carry, same + here * (centre * here), cross + here * (centre * value)
 
-        carry, same, cross = lax.fori_loop(0, ROWS, inner, (carry, zero, zero), unroll=4)
+        carry, same, cross = lax.fori_loop(0, ROWS, inner, (carry, zero, zero), unroll=16)
         moments += [same, cross]
         for a in range(HALO + ROWS, last + 1):
             carry, _, _ = advance_row(a, carry)
@@ -495,7 +558,7 @@
         h_out[:, tile(t)] = joined(here, ahead)
         return ahead, beyond
 
-    lax.fori_loop(0, PAIRS, slopes, (level_row(HALO - 1), level_row(HALO)), unroll=2)
+    lax.fori_loop(0, PAIRS, slopes, (level_row(HALO - 1), level_row(HALO)), unroll=8)
     for copy in out_copies:
         copy.wait()
 
@@ -522,6 +585,7 @@
         in_specs=[wide] * 4 + [thin] * 3,
         out_specs=[wide] * 4 + [thin],
         out_shape=[big] * 4 + [small],
+        compiler_params=pltpu.CompilerParams(vmem_limit_bytes=16 * 1024 * 1024),
         name="finish",
     )(*fields, *extras)
 
@@ -532,6 +596,7 @@
     big = jax.ShapeDtypeStruct((stacked, CELLS), F32)
     small = jax.ShapeDtypeStruct((SLOTS, CELLS), F32)
     anywhere = pl.BlockSpec(memory_space=pl.ANY)
+    held = pl.BlockSpec(memory_space=pltpu.HBM)
     vmem = pl.BlockSpec(memory_space=pltpu.VMEM)
     dma = pltpu.SemaphoreType.DMA
     far_count = sizes[0] * sizes[1] // NEAR
@@ -539,19 +604,26 @@
     results = pl.pallas_call(
         functools.partial(kernel, sizes),
         out_shape=[big] * 4 + [small] * 3,
-        in_specs=[anywhere] * 7 + [pl.BlockSpec(memory_space=pltpu.SMEM), anywhere],
+        in_specs=[held] * 9,
         out_specs=[anywhere] * 4 + [vmem] * 3,
         scratch_shapes=[
-            pltpu.VMEM((4, stacked, CELLS + 2 * LANES), F32),
+            pltpu.VMEM((4, stacked, CELLS), F32),
             pltpu.VMEM((stacked - SLOTS, CELLS), F32),
             pltpu.VMEM((SLOTS, CELLS), F32),
             pltpu.VMEM((SLOTS, CELLS), F32),
-            pltpu.VMEM((SLOTS, 8), jnp.int32),
+            pltpu.VMEM((8, LANES), jnp.int32),
+            pltpu.SMEM((SLOTS * far_count * NEAR,), jnp.int32),
             pltpu.VMEM((4, stacked, CELLS), F32),
             pltpu.VMEM((stacked, CELLS), F32),
             pltpu.VMEM((stacked, CELLS), F32),
             pltpu.VMEM((stacked, CELLS), F32),
             pltpu.VMEM((4, stacked, LANES), F32),
+            pltpu.VMEM((4, stacked, CELLS), F32),
+            pltpu.VMEM((4, stacked, CELLS), F32),
+            pltpu.VMEM((4, stacked, CELLS + 2 * LANES), F32),
+            pltpu.VMEM((4, stacked, CELLS), F32),
+            pltpu.VMEM((2 * LANES, 4 * LANES), BF16),
+            pltpu.VMEM((2 * LANES, LANES), BF16),
             pltpu.VMEM((4, 2, stacked, LANES), F32),
             pltpu.VMEM((2, 4, 2, stacked, LANES), F32),
             pltpu.VMEM((8, SLOTS, LANES), F32),
@@ -563,13 +635,16 @@
             pltpu.VMEM((tall, SLOTS, LANES), F32),
             pltpu.VMEM((tall, SLOTS, LANES), F32),
             pltpu.VMEM((ROWS, SLOTS, LANES), F32),
-            pltpu.VMEM((4, tall, SLOTS, LANES), F32),
+            pltpu.VMEM((tall, SLOTS, LANES), F32),
+            pltpu.VMEM((tall, SLOTS, LANES), F32),
+            pltpu.VMEM((tall, SLOTS, LANES), F32),
+            pltpu.VMEM((tall, SLOTS, LANES), F32),
             pltpu.VMEM((4, SLOTS, LANES), F32),
             pltpu.VMEM((NEAR, SLOTS, LANES), F32),
             pltpu.VMEM((far_count, SLOTS, LANES), F32),
             pltpu.VMEM((NEAR, SLOTS, LANES), F32),
             pltpu.VMEM((far_count, SLOTS, LANES), F32),
-            dma((8,)),
+            dma((9,)),
             dma((4,)),
             dma((2, 4)),
             dma((2, 4)),
@@ -586,7 +661,12 @@
             collective_id=0, has_side_effects=True, vmem_limit_bytes=40 * 1024 * 1024
         ),
         name="ocean_step",
-    )(*fields, k.reshape(stacked - SLOTS, CELLS), c, g, flags, lists)
+    )(
+        *[
+            pltpu.with_memory_space_constraint(x, pltpu.HBM)
+            for x in (*fields, k.reshape(stacked - SLOTS, CELLS), c, g, flags, lists.T)
+        ],
+    )
     done = finish(results[:4], results[4:])
     shape = (LEVELS, SLOTS, CELLS)
     return tuple(x.reshape(shape) for x in done[:4]) + (done[4],)

time: 76 us -> 45.7 us (0.60)
  Pallas kernels: 61.8 us -> 44.8 us
  local copies, waits for them, and re-layouts: 13 us -> 0 us
    pallas_call x1, Pallas kernels: 57 us -> 42.1 us  [local(): pl.pallas_call(functools.partial(kernel, sizes), out_shape=[big] * 4 + [s...]
    unnamed x31 -> x0, local copies, waits for them, and re-layouts: 13 us -> none
    pallas_call x1, Pallas kernels: 4.76 us -> 2.74 us  [finish(): pl.pallas_call(finish_kernel, grid=(chunks,), in_specs=[wide] * 4 + [thin...]
where the time goes in v2:
time: 45.7 us; the launch traced here: 45.4 us
  Pallas kernels  44.8 us (98%)
  between operations  0.64 us (1%)
    pallas_call x1, Pallas kernels, local(): pl.pallas_call(functools.partial(kernel, sizes), out_shape=[big] * 4 + [s...  42.1 us
    pallas_call x1, Pallas kernels, finish(): pl.pallas_call(finish_kernel, grid=(chunks,), in_specs=[wide] * 4 + [thin...  2.74 us

profile of v2, /device:TPU:0, one launch (start us, length us, event | category | flops | bytes accessed | tf_op | source)
XLA Modules:
  0.0 45.4 jit_solution(4088155897581878409)
XLA Ops:
  0.6 42.1 %ocean_step.1 = (f32[64,4096]{1,0:T(8,128)S(1)}, f32[64,4096]{1,0:T(8,128)S(1)}, f32[64,4096]{1,0:T(8,128)S(1)}, f32[64,4096]{1,0:T(8,128)S(1)}, f32[8,4096]{1,0...) custom-call(f32[64,4096]{1,0:T(8,128)} %bitcast.10, f32[64,4096]{1,0:T(8,128)} %bitcast.11, ...), custom_call_target="tpu_custom_call" | custom-call | tf_op jit(solution)/shard_map/ocean_step/pallas_call | solution.py:604
  42.7 2.7 %finish.1 = (f32[64,4096]{1,0:T(8,128)}, f32[64,4096]{1,0:T(8,128)}, f32[64,4096]{1,0:T(8,128)}, f32[64,4096]{1,0:T(8,128)}, f32[8,4096]{1,0:T(8,128)}) custom-call(f32[64,4096]{1,0:T(8,128)S(1)} %get-tuple-element.17.t_in, f32[64,4096]{1,0:T(8,128)S(1)} %get-tuple-element.18.s_in, f32[64,4096]{1,0:T(8,128)S(1)} %get-tuple-element.19.u_in, ...), custom_call_target="tpu_custom_call" | custom-call | tf_op jit(solution)/shard_map/finish/pallas_call | solution.py:582

commit v3 on v2

v3 whole, which is shorter than its diff:
```python
import functools
import itertools

import jax
import jax.numpy as jnp
from jax import lax
from jax.experimental import pallas as pl
from jax.experimental.pallas import tpu as pltpu
from jax.sharding import PartitionSpec as P

MESH = pl.DeviceIdType.MESH
F32 = jnp.float32
BF16 = jnp.bfloat16
LANES = 128
SLOTS = 8
LEVELS = 8
PAIRS = 32
CELLS = 4096
ROWS = 64
HALO = 4
CHUNK = 8
PARTS = 4


def tile(t):
    return pl.ds(pl.multiple_of(t * LANES, LANES), LANES)


def kernel(
    sizes,
    t_in, s_in, u_in, v_in, k_in, c_in, g_in, flags_in, lists,
    t_out, s_out, u_out, v_out, sx_out, sy_out, h_out,
    q, kk, cc, src, own_lists, flags, mixed, ip, fu, gl, hx,
    east_of, west_of, half_of, edge_of, shifts, spread,
    strips, arrived, mstrips, marrived, zstrips, zarrived,
    z2, mi2, zx, mx, mrow, v1, v2, v3, v4, inward, choose, part, near_sums, far_sums,
    in_sem, out_sem, strip_send, strip_recv, m_send, m_recv, z_send, z_recv, sum_send, sum_recv,
):
    count_x, count_y = sizes
    total = count_x * count_y
    gx, gy = lax.axis_index("gx"), lax.axis_index("gy")
    pos = gx * count_y + gy
    before, after = (pos + total - 1) % total, (pos + 1) % total
    ring = [(before // count_y, before % count_y), (after // count_y, after % count_y)]

    ys = [(gx + n) % 4 for n in range(4)]
    zs = [(gy // 8 + n) % 4 * 8 for n in range(4)]
    xs = [(gy // 2 + n) % 4 * 2 for n in range(4)]
    cores = [(gy + n) % 2 for n in range(2)]

    def hops(step):
        return -sum(min(n, 4 - n) for n in step)

    near_steps = sorted(itertools.product((0, 2, 1, 3), range(2)), key=lambda step: hops(step[:1]))
    far_steps = sorted(itertools.product(range(4), range(4)), key=hops)
    near = [(gx, zs[0] + xs[x] + cores[c]) for x, c in near_steps if x or c]
    far = [(ys[y], zs[z] + xs[0] + cores[0]) for y, z in far_steps if y or z]
    groups = ((near, gy % 8), (far, gx * 4 + gy // 8))
    partners = ring + near + far

    barrier = pltpu.get_barrier_semaphore()

    loads = []
    for number, ref in enumerate((t_in, s_in, u_in, v_in)):
        loads.append(pltpu.make_async_copy(ref, q.at[number], in_sem.at[number]))
    loads.append(pltpu.make_async_copy(
            lists.at[:, tile(pos // (LANES // SLOTS))], own_lists, in_sem.at[4]
        ))
    loads.append(pltpu.make_async_copy(c_in, cc, in_sem.at[5]))
    loads.append(pltpu.make_async_copy(k_in, kk, in_sem.at[6]))
    loads.append(pltpu.make_async_copy(g_in, src, in_sem.at[7]))
    for load in loads:
        load.start()
    flag_load = pltpu.make_async_copy(flags_in, flags, in_sem.at[8])
    flag_load.start()
    for other in partners:
        pl.semaphore_signal(barrier, inc=1, device_id=other, device_id_type=MESH)

    lane = lax.broadcasted_iota(jnp.int32, (SLOTS, LANES), 1)
    slot = lax.broadcasted_iota(jnp.int32, (SLOTS, LANES), 0)
    low_half = lane < ROWS
    lane_all = lax.broadcasted_iota(jnp.int32, (LEVELS * SLOTS, LANES), 1)

    def send_strips(number):
        copies = []
        for side in range(2):
            copy = pltpu.make_async_remote_copy(
                src_ref=strips.at[number],
                dst_ref=arrived.at[1 - side, number],
                send_sem=strip_send.at[side, number],
                recv_sem=strip_recv.at[1 - side, number],
                device_id=ring[side],
                device_id_type=MESH,
            )
            copy.start()
            copies.append(copy)
        return copies

    row = lax.broadcasted_iota(jnp.int32, (2 * LANES, LANES), 0) % LANES
    column = lax.broadcasted_iota(jnp.int32, (2 * LANES, LANES), 1)
    odd = column % 2 == 1
    upper_odd = (column >= 63) & (column < 127)
    packing = jnp.where(
        odd, jnp.where(upper_odd, 63, 127), jnp.where(column < ROWS, 0, ROWS)
    )
    edge_row = row % 2 == 1
    target = jnp.where(
        edge_row,
        jnp.where((row >= 63) & (row < 127), 0, ROWS),
        jnp.where(row < ROWS, 63, 127),
    )
    for place, chosen_lanes in enumerate(
        (
            (row == column + 1) & (column % ROWS != ROWS - 1),
            (row == column - 1) & (column % ROWS != 0),
            row == (column + ROWS) % LANES,
            row == packing,
        )
    ):
        shifts[:, place * LANES : (place + 1) * LANES] = jnp.where(chosen_lanes, 1.0, 0.0).astype(BF16)
    spread[...] = jnp.where(column == target, 1.0, 0.0).astype(BF16)

    position = lax.broadcasted_iota(jnp.int32, (16, 2 * LANES), 1)
    for t in range(PAIRS):
        choose[t] = jnp.where((((position + 1) & 63) >> 1) == t, 1.0, 0.0).astype(BF16)

    def parts(value):
        high = value.astype(BF16)
        rest = (value - high.astype(F32)).astype(BF16)
        return jnp.concatenate([high, rest], axis=1)

    stacked = LEVELS * SLOTS
    strip_copies = [None] * 4

    def shift_field(number):
        def shift_all(chunk, acc):
            first = chunk * CHUNK
            pieces = []
            for i in range(CHUNK):
                value = q[number, :, tile(first + i)]
                if number == 0:
                    value = value - q[1, :, tile(first + i)]
                    q[0, :, tile(first + i)] = value
                pieces.append(parts(value))
            split_parts = jnp.concatenate(pieces, axis=0)
            moved = jnp.dot(split_parts, shifts[...], preferred_element_type=F32)
            for i in range(CHUNK):
                rows = slice(i * stacked, (i + 1) * stacked)
                east_of[number, :, tile(first + i)] = moved[rows, :LANES]
                west_of[number, :, tile(first + i)] = moved[rows, LANES : 2 * LANES]
                half_of[number, :, tile(first + i + 1)] = moved[rows, 2 * LANES : 3 * LANES]
                here = (((lane_all + 1) & 63) >> 1) == first + i
                acc = jnp.where(here, moved[rows, 3 * LANES :], acc)
            return acc

        strips[number, 0] = lax.fori_loop(
            0, PAIRS // CHUNK, shift_all, jnp.zeros((stacked, LANES), F32)
        )
        for t in (0, PAIRS + 1):
            half_of[number, :, tile(t)] = jnp.zeros((stacked, LANES), F32)
        strips[number, 1] = jnp.where(
            lane_all < ROWS, q[number, :, tile(0)], q[number, :, tile(PAIRS - 1)]
        )
        strip_copies[number] = send_strips(number)

    loads[0].wait()
    loads[1].wait()
    pl.semaphore_wait(barrier, len(partners))
    shift_field(0)

    flag_load.wait()
    weight = jnp.zeros((SLOTS, LANES), F32)
    for b in range(SLOTS):
        flag = jnp.where(flags[pos * SLOTS + b] > 0, 1.0, 0.0)
        weight = jnp.where(slot == b, flag, weight)

    loads[4].wait()
    loads[5].wait()

    def wide_strips(value_of, store):
        for group in range(4):
            packed = jnp.zeros((SLOTS, LANES), F32)
            for k in range(8):
                value = value_of[8 * group + k]
                moved = pltpu.roll(value, 8 * k, 1) if k else value
                packed = jnp.where((((lane + 4) & 63) >> 3) == k, moved, packed)
            store[group] = packed
        for place, t in enumerate((0, 1, PAIRS - 2, PAIRS - 1)):
            store[4 + place] = value_of[t]

    def diagonal(t, _):
        centre = 6.0 + cc[:, tile(t)]
        mi2[t] = weight / centre
        mrow[2 * t] = jnp.where(low_half, centre, 0.0)
        mrow[2 * t + 1] = jnp.where(low_half, pltpu.roll(centre, 64, 1), 0.0)
        return 0

    lax.fori_loop(0, PAIRS, diagonal, 0, unroll=8)
    wide_strips(mi2, mstrips)

    def exchange(store, landing, send_sem, recv_sem):
        copies = []
        for side in range(2):
            copy = pltpu.make_async_remote_copy(
                src_ref=store,
                dst_ref=landing.at[1 - side],
                send_sem=send_sem.at[side],
                recv_sem=recv_sem.at[1 - side],
                device_id=ring[side],
                device_id_type=MESH,
            )
            copy.start()
            copies.append(copy)
        return copies

    m_copies = exchange(mstrips, marrived, m_send, m_recv)

    listed_lanes = pltpu.roll(
        own_lists[...].astype(F32), (LANES - (pos % (LANES // SLOTS)) * SLOTS) % LANES, 1
    )
    chosen = []
    for direction in range(8):
        line = jnp.broadcast_to(listed_lanes[direction : direction + 1], (SLOTS, LANES))
        own = jnp.sum(jnp.where(lane == slot, line, 0.0), axis=1, keepdims=True)
        listed = jnp.broadcast_to(own, (SLOTS, LANES)).astype(jnp.int32)
        column = (listed - (pos - 1) * SLOTS + total * SLOTS) % (total * SLOTS)
        there = listed >= 0
        which = column // SLOTS
        row = jnp.where(there, column % SLOTS, 0)
        chosen.append((row, [there & (which == side) for side in range(3)]))

    def take(direction, sources):
        row, sides = chosen[direction]
        result = jnp.zeros((SLOTS, LANES), F32)
        for source, side in zip(sources, sides):
            result = jnp.where(side, jnp.take_along_axis(source, row, axis=0), result)
        return result

    east_edge = (lane & 63) == 63
    west_edge = (lane & 63) == 0

    def inside(numbers, t):
        total_gap = jnp.zeros((SLOTS, LANES), F32)
        for level in range(LEVELS):
            rows = pl.ds(level * SLOTS, SLOTS)
            zonal = q[2, rows, tile(t)]
            meridional = q[3, rows, tile(t)]
            from_west = zonal > 0.0
            from_south = meridional > 0.0
            behind = low_half & from_south
            beyond = jnp.logical_not(low_half | from_south)
            speed_x = jnp.abs(zonal)
            speed_y = jnp.abs(meridional)
            stay = 1.0 - speed_x - speed_y
            if 0 in numbers:
                outside = (east_edge & jnp.logical_not(from_west)) | (west_edge & from_west)
                inward[rows, tile(t)] = jnp.where(outside, speed_x, 0.0)
            for number in numbers:
                along = jnp.where(from_west, west_of[number, rows, tile(t)], east_of[number, rows, tile(t)])
                across = jnp.where(beyond, half_of[number, rows, tile(t + 2)], half_of[number, rows, tile(t + 1)])
                across = jnp.where(behind, half_of[number, rows, tile(t)], across)
                moved = stay * q[number, rows, tile(t)] + speed_x * along + speed_y * across
                east_of[number, rows, tile(t)] = moved
                if number == 0:
                    total_gap = total_gap + moved
        return total_gap

    for i in (2, 3, 7):
        loads[i].wait()

    def first_load(t, _):
        z2[t] = src[:, tile(t)] + inside((0,), t) * (1.0 / LEVELS)
        return 0

    lax.fori_loop(0, PAIRS, first_load, 0)

    def share(use, group, value):
        phase = 2 * use + group
        peers, own = groups[group]
        store, landing = part.at[phase], (near_sums, far_sums)[group].at[use]
        store[0:1] = value
        landing[pl.ds(own, 1)] = value
        for peer in peers:
            pltpu.make_async_remote_copy(
                src_ref=store.at[pl.ds(0, 1)],
                dst_ref=landing.at[pl.ds(own, 1)],
                send_sem=sum_send.at[phase],
                recv_sem=sum_recv.at[phase],
                device_id=peer,
                device_id_type=MESH,
            ).start()

    def gather_sum(use, group):
        phase = 2 * use + group
        peers, _ = groups[group]
        landing = (near_sums, far_sums)[group].at[use]
        every = landing.at[pl.ds(0, len(peers))]
        copies = pltpu.make_async_remote_copy(
            src_ref=every,
            dst_ref=every,
            send_sem=sum_send.at[phase],
            recv_sem=sum_recv.at[phase],
            device_id=ring[0],
            device_id_type=MESH,
        )
        copies.wait_recv()
        copies.wait_send()
        return jnp.sum(landing[...], axis=0, keepdims=True)

    def spread_out(sums):
        return [jnp.broadcast_to(sums[:, i : i + 1], (SLOTS, LANES)) for i in range(8)]

    def gathered(values):
        result = jnp.zeros((SLOTS, LANES), F32)
        for place, value in enumerate(values):
            result = jnp.where(slot == place, jnp.sum(value, axis=0, keepdims=True), result)
        column = jnp.sum(result, axis=1, keepdims=True)
        return jnp.sum(jnp.where(lane == slot, column, 0.0), axis=0, keepdims=True)

    zero = jnp.zeros((SLOTS, LANES), F32)

    def split(t, carry):
        last, line, norm, product = carry
        value = z2[t] * mi2[t]
        for row, moved in ((2 * t, value), (2 * t + 1, pltpu.roll(value, 64, 1))):
            here = jnp.where(low_half, moved, 0.0)
            ahead = pltpu.roll(here, LANES - 1, 1)
            wide = here + 0.5 * (ahead + pltpu.roll(here, 1, 1))
            norm = norm + here * here * mrow[row]
            product = product + (here * ahead + last * wide)
            last = here
        return last, line, norm, product

    _, _, norm, product = lax.fori_loop(0, PAIRS, split, (zero, zero, zero, zero), unroll=8)
    share(0, 0, gathered([norm, 2.0 * product]))

    for number in (1, 2, 3):
        shift_field(number)
    share(0, 1, gather_sum(0, 0))

    def fill_halos(number):
        for copy in strip_copies[number]:
            copy.wait()

        for level in range(LEVELS):
            rows = pl.ds(level * SLOTS, SLOTS)
            sides = [arrived[0, number, 0, rows], strips[number, 0, rows], arrived[1, number, 0, rows]]
            hx[number, rows] = jnp.where((lane & 1) == 1, take(1, sides), take(0, sides))
            ends = [arrived[0, number, 1, rows], strips[number, 1, rows], arrived[1, number, 1, rows]]
            end = jnp.where(low_half, take(2, ends), take(3, ends))
            end = pltpu.roll(end, 64, 1)
            first = q[3, rows, tile(0)]
            last = q[3, rows, tile(PAIRS - 1)]
            below = jnp.where(low_half & (first > 0.0), first, 0.0) * end
            above = jnp.where(low_half | (last > 0.0), 0.0, -last) * end
            east_of[number, rows, tile(0)] += below
            east_of[number, rows, tile(PAIRS - 1)] += above
            if number == 0:
                z2[0] += below * (1.0 / LEVELS)
                z2[PAIRS - 1] += above * (1.0 / LEVELS)
        halo_parts = parts(hx[number])

        for chunk in range(PAIRS // CHUNK):
            first = chunk * CHUNK
            pieces = []
            for i in range(CHUNK):
                pieces += [halo_parts[16 * j : 16 * j + 16] * choose[first + i] for j in range(4)]
            found = jnp.dot(
                jnp.concatenate(pieces, axis=0), spread[...], preferred_element_type=F32
            )
            for i in range(CHUNK):
                edge_of[number, :, tile(first + i)] = found[i * stacked : (i + 1) * stacked]

    def advance(numbers, t):
        carried = {number: [] for number in numbers}
        for level in range(LEVELS):
            rows = pl.ds(level * SLOTS, SLOTS)
            inverse = ip[rows, tile(t)]
            entering = inward[rows, tile(t)]
            for number in numbers:
                moved = east_of[number, rows, tile(t)] + entering * edge_of[number, rows, tile(t)]
                value = moved * inverse
                if level > 0:
                    value = value + gl[rows, tile(t)] * carried[number][-1]
                carried[number].append(value)
        solved = {}
        for number in numbers:
            values = carried[number]
            for level in range(LEVELS - 2, -1, -1):
                rows = pl.ds(level * SLOTS, SLOTS)
                values[level] = values[level] + fu[rows, tile(t)] * values[level + 1]
            solved[number] = values
        for number in numbers:
            for level in range(LEVELS):
                value = solved[number][level]
                if number == 0:
                    value = value + solved[1][level]
                mixed[number, pl.ds(level * SLOTS, SLOTS), tile(t)] = value

    outs = (t_out, s_out, u_out, v_out)

    def write_out(number):
        copy = pltpu.make_async_copy(mixed.at[number], outs[number], out_sem.at[number])
        copy.start()
        return copy

    fill_halos(0)

    def whole_load(t, _):
        entering = jnp.zeros((SLOTS, LANES), F32)
        for level in range(LEVELS):
            rows = pl.ds(level * SLOTS, SLOTS)
            entering = entering + inward[rows, tile(t)] * edge_of[0, rows, tile(t)]
        z2[t] = (z2[t] + entering * (1.0 / LEVELS)) * mi2[t]
        return 0

    lax.fori_loop(0, PAIRS, whole_load, 0, unroll=4)
    wide_strips(z2, zstrips)
    z_copies = exchange(zstrips, zarrived, z_send, z_recv)

    def others_inside(t, _):
        inside((1, 2, 3), t)
        return 0

    lax.fori_loop(0, PAIRS, others_inside, 0)
    loads[6].wait()

    def factor(t, _):
        above = None
        for level in range(LEVELS):
            rows = pl.ds(level * SLOTS, SLOTS)
            pivot = 1.0
            if level > 0:
                lower = kk[pl.ds((level - 1) * SLOTS, SLOTS), tile(t)]
                pivot = pivot + lower
            if level < LEVELS - 1:
                upper = kk[rows, tile(t)]
                pivot = pivot + upper
            if level > 0:
                pivot = pivot - lower * above
            inverse = 1.0 / pivot
            ip[rows, tile(t)] = inverse * weight
            if level > 0:
                gl[rows, tile(t)] = lower * inverse
            if level < LEVELS - 1:
                above = upper * inverse
                fu[rows, tile(t)] = above
        return 0

    lax.fori_loop(0, PAIRS, factor, 0, unroll=2)


    def widen(store, landing, halves, wide, interior):
        def sources(place):
            return [landing[0, place], store[place], landing[1, place]]

        for first, directions, places in (
            (0, (3, 6, 7), (6, 7)),
            (HALO + ROWS, (2, 4, 5), (4, 5)),
        ):
            for i, place in enumerate(places):
                line = take(directions[0], sources(place))
                corner = jnp.where(
                    (lane & 63) < 32,
                    take(directions[1], sources(place)),
                    take(directions[2], sources(place)),
                )
                wide[first + 2 * i] = jnp.where(low_half, line, pltpu.roll(corner, 64, 1))
                wide[first + 2 * i + 1] = jnp.where(low_half, pltpu.roll(line, 64, 1), corner)
        for group in range(4):
            halves[group] = jnp.where(
                (lane & 4) == 0, take(0, sources(group)), take(1, sources(group))
            )

        def rows(t, _):
            side = halves[t // 8]
            step = (8 * t) % ROWS
            even, odd = interior(t)
            wide[HALO + 2 * t] = jnp.where(low_half, even, pltpu.roll(side, 64 - step, 1))
            wide[HALO + 2 * t + 1] = jnp.where(
                low_half, odd, pltpu.roll(side, (LANES - step) % LANES, 1)
            )
            return 0

        lax.fori_loop(0, PAIRS, rows, 0, unroll=8)

    for copy in m_copies:
        copy.wait()
    widen(mstrips, marrived, v1, mx, lambda t: (mi2[t], pltpu.roll(mi2[t], 64, 1)))
    for copy in z_copies:
        copy.wait()
    widen(
        zstrips, zarrived, v1, zx,
        lambda t: (z2[t], pltpu.roll(z2[t], 64, 1)),
    )

    def neighbours(value):
        paired = pltpu.roll(value, 1, 1) + pltpu.roll(value, LANES - 1, 1)
        return paired, value + 0.5 * paired

    basis = [zx, v1, v2, v3, v4]
    moments = []
    shift = None
    for power in range(4):
        old, new = basis[power], basis[power + 1]
        first, last = 1 + power, HALO + ROWS + 2 - power
        def read(a, power=power, old=old, shift=shift):
            value = old[a]
            if power:
                value = value - shift * basis[power - 1][a]
                old[a] = value
            return value

        def advance_row(a, carry, new=new, read=read):
            here, paired, wide, behind = carry
            ahead = read(a + 1)
            ahead_paired, ahead_wide = neighbours(ahead)
            value = mx[a] * (paired + behind + ahead_wide)
            new[a] = value
            return (ahead, ahead_paired, ahead_wide, wide), here, value

        behind = read(first - 1)
        here = read(first)
        carry = (here, *neighbours(here), neighbours(behind)[1])
        for a in range(first, HALO):
            carry, _, _ = advance_row(a, carry)

        def inner(r, state, power=power, advance_row=advance_row, shift=shift):
            carry, same, cross = state
            carry, here, value = advance_row(r + HALO, carry)
            weighed = mrow[r] * here
            if power == 0:
                return carry, same + here * weighed, cross
            if power == 3:
                value = value - shift * here
                return carry, same + here * weighed, (cross[0] + basis[2][r + HALO] * weighed, cross[1] + weighed * value)
            return carry, same + here * weighed, cross + basis[power - 1][r + HALO] * weighed

        start = (zero, zero) if power == 3 else zero
        carry, same, cross = lax.fori_loop(0, ROWS, inner, (carry, zero, start), unroll=16)
        if power:
            moments.append(cross[0] if power == 3 else cross)
        moments.append(same)
        if power == 3:
            moments.append(cross[1])
        for a in range(HALO + ROWS, last + 1):
            carry, _, _ = advance_row(a, carry)
        if power == 0:
            both = spread_out(gather_sum(0, 1))
            shift = both[1] / both[0]

    share(1, 0, gathered(moments))
    for number in (1, 2, 3):
        fill_halos(number)

    def tracers(t, _):
        advance((0, 1), t)
        return 0

    lax.fori_loop(0, PAIRS, tracers, 0)
    out_copies = [write_out(0), write_out(1)]
    share(1, 1, gather_sum(1, 0))

    def velocities(t, _):
        advance((2, 3), t)
        return 0

    lax.fori_loop(0, PAIRS, velocities, 0)
    out_copies += [write_out(2), write_out(3)]
    mu = spread_out(gather_sum(1, 1))

    rest = 1.0 - shift
    matrix = [[rest * mu[i + j] - mu[i + j + 1] for j in range(4)] for i in range(4)]
    lower = [[None] * 4 for _ in range(4)]
    pivots, inverses, ahead = [], [], []
    for j in range(4):
        pivot = matrix[j][j]
        for i in range(j):
            pivot = pivot - lower[j][i] * lower[j][i] * pivots[i]
        kept = pivot > 1e-6 * matrix[j][j]
        pivots.append(jnp.where(kept, pivot, 0.0) if j else pivot)
        inverses.append(jnp.where(kept, 1.0 / pivot, 0.0) if j else 1.0 / pivot)
        for i in range(j + 1, 4):
            entry = matrix[i][j]
            for m in range(j):
                entry = entry - lower[i][m] * lower[j][m] * pivots[m]
            lower[i][j] = entry * inverses[j]
        right = mu[j]
        for i in range(j):
            right = right - lower[j][i] * ahead[i]
        ahead.append(right)
    factors = [None] * 4
    for j in range(3, -1, -1):
        value = ahead[j] * inverses[j]
        for i in range(j + 1, 4):
            value = value - lower[i][j] * factors[i]
        factors[j] = value

    def level_row(a):
        value = factors[0] * basis[0][a]
        for j in range(1, 4):
            value = value + factors[j] * basis[j][a]
        return value

    def slopes(t, carry):
        behind, here = carry
        ahead = level_row(HALO + 2 * t + 1)
        beyond = level_row(HALO + 2 * t + 2)

        def zonal_slope(value):
            return 0.5 * (pltpu.roll(value, LANES - 1, 1) - pltpu.roll(value, 1, 1))

        def joined(even, odd):
            return jnp.where(low_half, even, pltpu.roll(odd, 64, 1))

        sx_out[:, tile(t)] = joined(zonal_slope(here), zonal_slope(ahead))
        sy_out[:, tile(t)] = joined(0.5 * (ahead - behind), 0.5 * (beyond - here))
        h_out[:, tile(t)] = joined(here, ahead)
        return ahead, beyond

    lax.fori_loop(0, PAIRS, slopes, (level_row(HALO - 1), level_row(HALO)), unroll=8)
    for copy in out_copies:
        copy.wait()


def finish_kernel(t_in, s_in, u_in, v_in, sx, sy, h, t_out, s_out, u_out, v_out, h_out, u, v, sems):
    copies = [
        pltpu.make_async_copy(source, target, sems.at[i])
        for i, (source, target) in enumerate(((t_in, t_out), (s_in, s_out), (h, h_out)))
    ]
    for copy in copies:
        copy.start()
    width = CELLS // PARTS
    for i in range(PARTS):
        columns = pl.ds(i * width, width)
        for n, (source, slope, store, target) in enumerate(
            ((u_in, sx, u, u_out), (v_in, sy, v, v_out))
        ):
            for level in range(LEVELS):
                rows = pl.ds(level * SLOTS, SLOTS)
                store[rows, columns] = source[rows, columns] - slope[:, columns]
            copy = pltpu.make_async_copy(
                store.at[:, columns], target.at[:, columns], sems.at[3 + 2 * i + n]
            )
            copy.start()
            copies.append(copy)
    for copy in copies:
        copy.wait()


def finish(fields, extras):
    vmem = pl.BlockSpec(memory_space=pltpu.VMEM)
    hbm = pl.BlockSpec(memory_space=pltpu.HBM)
    big = jax.ShapeDtypeStruct((LEVELS * SLOTS, CELLS), F32)
    small = jax.ShapeDtypeStruct((SLOTS, CELLS), F32)
    return pl.pallas_call(
        finish_kernel,
        in_specs=[vmem] * 7,
        out_specs=[hbm] * 5,
        out_shape=[big] * 4 + [small],
        scratch_shapes=[
            pltpu.VMEM((LEVELS * SLOTS, CELLS), F32),
            pltpu.VMEM((LEVELS * SLOTS, CELLS), F32),
            pltpu.SemaphoreType.DMA((3 + 2 * PARTS,)),
        ],
        compiler_params=pltpu.CompilerParams(vmem_limit_bytes=16 * 1024 * 1024),
        name="finish",
    )(*fields, *extras)


def local(sizes, t, s, u, v, k, c, g, flags, lists):
    stacked = LEVELS * SLOTS
    fields = [x.reshape(stacked, CELLS) for x in (t, s, u, v)]
    big = jax.ShapeDtypeStruct((stacked, CELLS), F32)
    small = jax.ShapeDtypeStruct((SLOTS, CELLS), F32)
    anywhere = pl.BlockSpec(memory_space=pl.ANY)
    held = pl.BlockSpec(memory_space=pltpu.HBM)
    vmem = pl.BlockSpec(memory_space=pltpu.VMEM)
    dma = pltpu.SemaphoreType.DMA
    total = sizes[0] * sizes[1]
    tall = ROWS + 2 * HALO
    results = pl.pallas_call(
        functools.partial(kernel, sizes),
        out_shape=[big] * 4 + [small] * 3,
        in_specs=[held] * 9,
        out_specs=[anywhere] * 4 + [vmem] * 3,
        scratch_shapes=[
            pltpu.VMEM((4, stacked, CELLS), F32),
            pltpu.VMEM((stacked - SLOTS, CELLS), F32),
            pltpu.VMEM((SLOTS, CELLS), F32),
            pltpu.VMEM((SLOTS, CELLS), F32),
            pltpu.VMEM((8, LANES), jnp.int32),
            pltpu.SMEM((SLOTS * total,), jnp.int32),
            pltpu.VMEM((4, stacked, CELLS), F32),
            pltpu.VMEM((stacked, CELLS), F32),
            pltpu.VMEM((stacked, CELLS), F32),
            pltpu.VMEM((stacked, CELLS), F32),
            pltpu.VMEM((4, stacked, LANES), F32),
            pltpu.VMEM((4, stacked, CELLS), F32),
            pltpu.VMEM((4, stacked, CELLS), F32),
            pltpu.VMEM((4, stacked, CELLS + 2 * LANES), F32),
            pltpu.VMEM((4, stacked, CELLS), F32),
            pltpu.VMEM((2 * LANES, 4 * LANES), BF16),
            pltpu.VMEM((2 * LANES, LANES), BF16),
            pltpu.VMEM((4, 2, stacked, LANES), F32),
            pltpu.VMEM((2, 4, 2, stacked, LANES), F32),
            pltpu.VMEM((8, SLOTS, LANES), F32),
            pltpu.VMEM((2, 8, SLOTS, LANES), F32),
            pltpu.VMEM((8, SLOTS, LANES), F32),
            pltpu.VMEM((2, 8, SLOTS, LANES), F32),
            pltpu.VMEM((PAIRS, SLOTS, LANES), F32),
            pltpu.VMEM((PAIRS, SLOTS, LANES), F32),
            pltpu.VMEM((tall, SLOTS, LANES), F32),
            pltpu.VMEM((tall, SLOTS, LANES), F32),
            pltpu.VMEM((ROWS, SLOTS, LANES), F32),
            pltpu.VMEM((tall, SLOTS, LANES), F32),
            pltpu.VMEM((tall, SLOTS, LANES), F32),
            pltpu.VMEM((tall, SLOTS, LANES), F32),
            pltpu.VMEM((tall, SLOTS, LANES), F32),
            pltpu.VMEM((stacked, CELLS), F32),
            pltpu.VMEM((PAIRS, 16, 2 * LANES), BF16),
            pltpu.VMEM((4, SLOTS, LANES), F32),
            pltpu.VMEM((2, 8, LANES), F32),
            pltpu.VMEM((2, 16, LANES), F32),
            dma((9,)),
            dma((4,)),
            dma((2, 4)),
            dma((2, 4)),
            dma((2,)),
            dma((2,)),
            dma((2,)),
            dma((2,)),
            dma((4,)),
            dma((4,)),
        ],
        compiler_params=pltpu.CompilerParams(
            collective_id=0, has_side_effects=True, vmem_limit_bytes=40 * 1024 * 1024
        ),
        name="ocean_step",
    )(
        *[
            pltpu.with_memory_space_constraint(x, pltpu.HBM)
            for x in (*fields, k.reshape(stacked - SLOTS, CELLS), c, g, flags, lists.T)
        ],
    )
    done = finish(results[:4], results[4:])
    shape = (LEVELS, SLOTS, CELLS)
    return tuple(x.reshape(shape) for x in done[:4]) + (done[4],)


def solution(mesh):
    whole = P(None, ("gx", "gy"), None)
    flat = P(("gx", "gy"), None)
    return jax.shard_map(
        functools.partial(local, (mesh.shape["gx"], mesh.shape["gy"])),
        mesh=mesh,
        in_specs=(whole, whole, whole, whole, whole, flat, flat, P(), P()),
        out_specs=(whole, whole, whole, whole, flat),
        check_vma=False,
    )
```

time: 45.7 us -> 36.3 us (0.79)
  Pallas kernels: 44.8 us -> 35.5 us
    pallas_call x1, Pallas kernels: 42.1 us -> 33.4 us  [local(): pl.pallas_call(functools.partial(kernel, sizes), out_shape=[big] * 4 + [s...]
    pallas_call x1, Pallas kernels: 2.74 us -> 2.14 us  [finish(): pl.pallas_call(finish_kernel, in_specs=[vmem] * 7, out_specs=[hbm] * 5, o...]
where the time goes in v3:
time: 36.3 us; the launch traced here: 36.2 us
  Pallas kernels  35.5 us (98%)
  between operations  0.64 us (2%)
    pallas_call x1, Pallas kernels, local(): pl.pallas_call(functools.partial(kernel, sizes), out_shape=[big] * 4 + [s...  33.4 us
    pallas_call x1, Pallas kernels, finish(): pl.pallas_call(finish_kernel, in_specs=[vmem] * 7, out_specs=[hbm] * 5, o...  2.14 us

profile of v3, /device:TPU:0, one launch (start us, length us, event | category | flops | bytes accessed | tf_op | source)
XLA Modules:
  0.0 36.2 jit_solution(3264431119785290181)
XLA Ops:
  0.6 33.4 %ocean_step.1 = (f32[64,4096]{1,0:T(8,128)S(1)}, f32[64,4096]{1,0:T(8,128)S(1)}, f32[64,4096]{1,0:T(8,128)S(1)}, f32[64,4096]{1,0:T(8,128)S(1)}, f32[8,4096]{1,0...) custom-call(f32[64,4096]{1,0:T(8,128)} %bitcast.10, f32[64,4096]{1,0:T(8,128)} %bitcast.11, ...), custom_call_target="tpu_custom_call" | custom-call | tf_op jit(solution)/shard_map/ocean_step/pallas_call | solution.py:682
  34.0 2.1 %finish.1 = (f32[64,4096]{1,0:T(8,128)}, f32[64,4096]{1,0:T(8,128)}, f32[64,4096]{1,0:T(8,128)}, f32[64,4096]{1,0:T(8,128)}, f32[8,4096]{1,0:T(8,128)}) custom-call(f32[64,4096]{1,0:T(8,128)S(1)} %get-tuple-element.17.t_in, f32[64,4096]{1,0:T(8,128)S(1)} %get-tuple-element.18.s_in, f32[64,4096]{1,0:T(8,128)S(1)} %get-tuple-element.19.u_in, ...), custom_call_target="tpu_custom_call" | custom-call | tf_op jit(solution)/shard_map/finish/pallas_call | solution.py:656

commit v4 on v3

--- a/solution.py
+++ b/solution.py
@@ -56,7 +56,7 @@
     near = [(gx, zs[0] + xs[x] + cores[c]) for x, c in near_steps if x or c]
     far = [(ys[y], zs[z] + xs[0] + cores[0]) for y, z in far_steps if y or z]
     groups = ((near, gy % 8), (far, gx * 4 + gy // 8))
-    partners = ring + near + far
+    partners = ring + far + near
 
     barrier = pltpu.get_barrier_semaphore()
 
@@ -69,12 +69,14 @@
     loads.append(pltpu.make_async_copy(c_in, cc, in_sem.at[5]))
     loads.append(pltpu.make_async_copy(k_in, kk, in_sem.at[6]))
     loads.append(pltpu.make_async_copy(g_in, src, in_sem.at[7]))
-    for load in loads:
+    for load in loads[:2]:
+        load.start()
+    for other in partners:
+        pl.semaphore_signal(barrier, inc=1, device_id=other, device_id_type=MESH)
+    for load in loads[2:]:
         load.start()
     flag_load = pltpu.make_async_copy(flags_in, flags, in_sem.at[8])
     flag_load.start()
-    for other in partners:
-        pl.semaphore_signal(barrier, inc=1, device_id=other, device_id_type=MESH)
 
     lane = lax.broadcasted_iota(jnp.int32, (SLOTS, LANES), 1)
     slot = lax.broadcasted_iota(jnp.int32, (SLOTS, LANES), 0)
@@ -154,19 +156,19 @@
             return acc
 
         strips[number, 0] = lax.fori_loop(
-            0, PAIRS // CHUNK, shift_all, jnp.zeros((stacked, LANES), F32)
+            0, PAIRS // CHUNK, shift_all, jnp.zeros((stacked, LANES), F32), unroll=2
         )
         for t in (0, PAIRS + 1):
             half_of[number, :, tile(t)] = jnp.zeros((stacked, LANES), F32)
         strips[number, 1] = jnp.where(
             lane_all < ROWS, q[number, :, tile(0)], q[number, :, tile(PAIRS - 1)]
         )
-        strip_copies[number] = send_strips(number)
 
     loads[0].wait()
     loads[1].wait()
+    shift_field(0)
     pl.semaphore_wait(barrier, len(partners))
-    shift_field(0)
+    strip_copies[0] = send_strips(0)
 
     flag_load.wait()
     weight = jnp.zeros((SLOTS, LANES), F32)
@@ -336,7 +338,6 @@
 
     for number in (1, 2, 3):
         shift_field(number)
-    share(0, 1, gather_sum(0, 0))
 
     def fill_halos(number):
         for copy in strip_copies[number]:
@@ -414,9 +415,12 @@
         z2[t] = (z2[t] + entering * (1.0 / LEVELS)) * mi2[t]
         return 0
 
-    lax.fori_loop(0, PAIRS, whole_load, 0, unroll=4)
+    lax.fori_loop(0, PAIRS, whole_load, 0, unroll=8)
     wide_strips(z2, zstrips)
     z_copies = exchange(zstrips, zarrived, z_send, z_recv)
+    for number in (1, 2, 3):
+        strip_copies[number] = send_strips(number)
+    share(0, 1, gather_sum(0, 0))
 
     def others_inside(t, _):
         inside((1, 2, 3), t)
@@ -482,7 +486,7 @@
             )
             return 0
 
-        lax.fori_loop(0, PAIRS, rows, 0, unroll=8)
+        lax.fori_loop(0, PAIRS, rows, 0, unroll=32)
 
     for copy in m_copies:
         copy.wait()
@@ -537,7 +541,7 @@
             return carry, same + here * weighed, cross + basis[power - 1][r + HALO] * weighed
 
         start = (zero, zero) if power == 3 else zero
-        carry, same, cross = lax.fori_loop(0, ROWS, inner, (carry, zero, start), unroll=16)
+        carry, same, cross = lax.fori_loop(0, ROWS, inner, (carry, zero, start), unroll=64)
         if power:
             moments.append(cross[0] if power == 3 else cross)
         moments.append(same)
@@ -618,7 +622,7 @@
         h_out[:, tile(t)] = joined(here, ahead)
         return ahead, beyond
 
-    lax.fori_loop(0, PAIRS, slopes, (level_row(HALO - 1), level_row(HALO)), unroll=8)
+    lax.fori_loop(0, PAIRS, slopes, (level_row(HALO - 1), level_row(HALO)), unroll=32)
     for copy in out_copies:
         copy.wait()
 

time: 36.3 us -> 31.5 us (0.87)
  Pallas kernels: 35.5 us -> 30.7 us
    pallas_call x1, Pallas kernels: 33.4 us -> 28.6 us  [local(): pl.pallas_call(functools.partial(kernel, sizes), out_shape=[big] * 4 + [s...]
where the time goes in v4:
time: 31.5 us; the launch traced here: 31.4 us
  Pallas kernels  30.7 us (97%)
  between operations  0.64 us (2%)
    pallas_call x1, Pallas kernels, local(): pl.pallas_call(functools.partial(kernel, sizes), out_shape=[big] * 4 + [s...  28.6 us
    pallas_call x1, Pallas kernels, finish(): pl.pallas_call(finish_kernel, in_specs=[vmem] * 7, out_specs=[hbm] * 5, o...  2.14 us

profile of v4, /device:TPU:0, one launch (start us, length us, event | category | flops | bytes accessed | tf_op | source)
XLA Modules:
  0.0 31.4 jit_solution(2381372620574791538)
XLA Ops:
  0.6 28.6 %ocean_step.1 = (f32[64,4096]{1,0:T(8,128)S(1)}, f32[64,4096]{1,0:T(8,128)S(1)}, f32[64,4096]{1,0:T(8,128)S(1)}, f32[64,4096]{1,0:T(8,128)S(1)}, f32[8,4096]{1,0...) custom-call(f32[64,4096]{1,0:T(8,128)} %bitcast.10, f32[64,4096]{1,0:T(8,128)} %bitcast.11, ...), custom_call_target="tpu_custom_call" | custom-call | tf_op jit(solution)/shard_map/ocean_step/pallas_call | solution.py:686
  29.2 2.1 %finish.1 = (f32[64,4096]{1,0:T(8,128)}, f32[64,4096]{1,0:T(8,128)}, f32[64,4096]{1,0:T(8,128)}, f32[64,4096]{1,0:T(8,128)}, f32[8,4096]{1,0:T(8,128)}) custom-call(f32[64,4096]{1,0:T(8,128)S(1)} %get-tuple-element.17.t_in, f32[64,4096]{1,0:T(8,128)S(1)} %get-tuple-element.18.s_in, f32[64,4096]{1,0:T(8,128)S(1)} %get-tuple-element.19.u_in, ...), custom_call_target="tpu_custom_call" | custom-call | tf_op jit(solution)/shard_map/finish/pallas_call | solution.py:660

commit v5 on v4

--- a/solution.py
+++ b/solution.py
@@ -156,7 +156,7 @@
             return acc
 
         strips[number, 0] = lax.fori_loop(
-            0, PAIRS // CHUNK, shift_all, jnp.zeros((stacked, LANES), F32), unroll=2
+            0, PAIRS // CHUNK, shift_all, jnp.zeros((stacked, LANES), F32), unroll=4
         )
         for t in (0, PAIRS + 1):
             half_of[number, :, tile(t)] = jnp.zeros((stacked, LANES), F32)
@@ -415,7 +415,7 @@
         z2[t] = (z2[t] + entering * (1.0 / LEVELS)) * mi2[t]
         return 0
 
-    lax.fori_loop(0, PAIRS, whole_load, 0, unroll=8)
+    lax.fori_loop(0, PAIRS, whole_load, 0, unroll=16)
     wide_strips(z2, zstrips)
     z_copies = exchange(zstrips, zarrived, z_send, z_recv)
     for number in (1, 2, 3):
@@ -427,6 +427,110 @@
         return 0
 
     lax.fori_loop(0, PAIRS, others_inside, 0)
+
+
+    def widen(store, landing, halves, wide, interior):
+        def sources(place):
+            return [landing[0, place], store[place], landing[1, place]]
+
+        for first, directions, places in (
+            (0, (3, 6, 7), (6, 7)),
+            (HALO + ROWS, (2, 4, 5), (4, 5)),
+        ):
+            for i, place in enumerate(places):
+                line = take(directions[0], sources(place))
+                corner = jnp.where(
+                    (lane & 63) < 32,
+                    take(directions[1], sources(place)),
+                    take(directions[2], sources(place)),
+                )
+                wide[first + 2 * i] = jnp.where(low_half, line, pltpu.roll(corner, 64, 1))
+                wide[first + 2 * i + 1] = jnp.where(low_half, pltpu.roll(line, 64, 1), corner)
+        for group in range(4):
+            halves[group] = jnp.where(
+                (lane & 4) == 0, take(0, sources(group)), take(1, sources(group))
+            )
+
+        def rows(t, _):
+            side = halves[t // 8]
+            step = (8 * t) % ROWS
+            even, odd = interior(t)
+            wide[HALO + 2 * t] = jnp.where(low_half, even, pltpu.roll(side, 64 - step, 1))
+            wide[HALO + 2 * t + 1] = jnp.where(
+                low_half, odd, pltpu.roll(side, (LANES - step) % LANES, 1)
+            )
+            return 0
+
+        lax.fori_loop(0, PAIRS, rows, 0, unroll=32)
+
+    for copy in m_copies:
+        copy.wait()
+    widen(mstrips, marrived, v1, mx, lambda t: (mi2[t], pltpu.roll(mi2[t], 64, 1)))
+    for copy in z_copies:
+        copy.wait()
+    widen(
+        zstrips, zarrived, v1, zx,
+        lambda t: (z2[t], pltpu.roll(z2[t], 64, 1)),
+    )
+
+    def neighbours(value):
+        paired = pltpu.roll(value, 1, 1) + pltpu.roll(value, LANES - 1, 1)
+        return paired, value + 0.5 * paired
+
+    basis = [zx, v1, v2, v3, v4]
+    moments = []
+    shift = None
+    for power in range(4):
+        old, new = basis[power], basis[power + 1]
+        first, last = 1 + power, HALO + ROWS + 2 - power
+        def read(a, power=power, old=old, shift=shift):
+            value = old[a]
+            if power:
+                value = value - shift * basis[power - 1][a]
+                old[a] = value
+            return value
+
+        def advance_row(a, carry, new=new, read=read):
+            here, paired, wide, behind = carry
+            ahead = read(a + 1)
+            ahead_paired, ahead_wide = neighbours(ahead)
+            value = mx[a] * (paired + behind + ahead_wide)
+            new[a] = value
+            return (ahead, ahead_paired, ahead_wide, wide), here, value
+
+        behind = read(first - 1)
+        here = read(first)
+        carry = (here, *neighbours(here), neighbours(behind)[1])
+        for a in range(first, HALO):
+            carry, _, _ = advance_row(a, carry)
+
+        def inner(r, state, power=power, advance_row=advance_row, shift=shift):
+            carry, same, cross = state
+            carry, here, value = advance_row(r + HALO, carry)
+            weighed = mrow[r] * here
+            if power == 0:
+                return carry, same + here * weighed, cross
+            if power == 3:
+                value = value - shift * here
+                return carry, same + here * weighed, (cross[0] + basis[2][r + HALO] * weighed, cross[1] + weighed * value)
+            return carry, same + here * weighed, cross + basis[power - 1][r + HALO] * weighed
+
+        start = (zero, zero) if power == 3 else zero
+        carry, same, cross = lax.fori_loop(0, ROWS, inner, (carry, zero, start), unroll=64)
+        if power:
+            moments.append(cross[0] if power == 3 else cross)
+        moments.append(same)
+        if power == 3:
+            moments.append(cross[1])
+        for a in range(HALO + ROWS, last + 1):
+            carry, _, _ = advance_row(a, carry)
+        if power == 0:
+            both = spread_out(gather_sum(0, 1))
+            shift = both[1] / both[0]
+
+    share(1, 0, gathered(moments))
+    fill_halos(1)
+
     loads[6].wait()
 
     def factor(t, _):
@@ -453,110 +557,6 @@
 
     lax.fori_loop(0, PAIRS, factor, 0, unroll=2)
 
-
-    def widen(store, landing, halves, wide, interior):
-        def sources(place):
-            return [landing[0, place], store[place], landing[1, place]]
-
-        for first, directions, places in (
-            (0, (3, 6, 7), (6, 7)),
-            (HALO + ROWS, (2, 4, 5), (4, 5)),
-        ):
-            for i, place in enumerate(places):
-                line = take(directions[0], sources(place))
-                corner = jnp.where(
-                    (lane & 63) < 32,
-                    take(directions[1], sources(place)),
-                    take(directions[2], sources(place)),
-                )
-                wide[first + 2 * i] = jnp.where(low_half, line, pltpu.roll(corner, 64, 1))
-                wide[first + 2 * i + 1] = jnp.where(low_half, pltpu.roll(line, 64, 1), corner)
-        for group in range(4):
-            halves[group] = jnp.where(
-                (lane & 4) == 0, take(0, sources(group)), take(1, sources(group))
-            )
-
-        def rows(t, _):
-            side = halves[t // 8]
-            step = (8 * t) % ROWS
-            even, odd = interior(t)
-            wide[HALO + 2 * t] = jnp.where(low_half, even, pltpu.roll(side, 64 - step, 1))
-            wide[HALO + 2 * t + 1] = jnp.where(
-                low_half, odd, pltpu.roll(side, (LANES - step) % LANES, 1)
-            )
-            return 0
-
-        lax.fori_loop(0, PAIRS, rows, 0, unroll=32)
-
-    for copy in m_copies:
-        copy.wait()
-    widen(mstrips, marrived, v1, mx, lambda t: (mi2[t], pltpu.roll(mi2[t], 64, 1)))
-    for copy in z_copies:
-        copy.wait()
-    widen(
-        zstrips, zarrived, v1, zx,
-        lambda t: (z2[t], pltpu.roll(z2[t], 64, 1)),
-    )
-
-    def neighbours(value):
-        paired = pltpu.roll(value, 1, 1) + pltpu.roll(value, LANES - 1, 1)
-        return paired, value + 0.5 * paired
-
-    basis = [zx, v1, v2, v3, v4]
-    moments = []
-    shift = None
-    for power in range(4):
-        old, new = basis[power], basis[power + 1]
-        first, last = 1 + power, HALO + ROWS + 2 - power
-        def read(a, power=power, old=old, shift=shift):
-            value = old[a]
-            if power:
-                value = value - shift * basis[power - 1][a]
-                old[a] = value
-            return value
-
-        def advance_row(a, carry, new=new, read=read):
-            here, paired, wide, behind = carry
-            ahead = read(a + 1)
-            ahead_paired, ahead_wide = neighbours(ahead)
-            value = mx[a] * (paired + behind + ahead_wide)
-            new[a] = value
-            return (ahead, ahead_paired, ahead_wide, wide), here, value
-
-        behind = read(first - 1)
-        here = read(first)
-        carry = (here, *neighbours(here), neighbours(behind)[1])
-        for a in range(first, HALO):
-            carry, _, _ = advance_row(a, carry)
-
-        def inner(r, state, power=power, advance_row=advance_row, shift=shift):
-            carry, same, cross = state
-            carry, here, value = advance_row(r + HALO, carry)
-            weighed = mrow[r] * here
-            if power == 0:
-                return carry, same + here * weighed, cross
-            if power == 3:
-                value = value - shift * here
-                return carry, same + here * weighed, (cross[0] + basis[2][r + HALO] * weighed, cross[1] + weighed * value)
-            return carry, same + here * weighed, cross + basis[power - 1][r + HALO] * weighed
-
-        start = (zero, zero) if power == 3 else zero
-        carry, same, cross = lax.fori_loop(0, ROWS, inner, (carry, zero, start), unroll=64)
-        if power:
-            moments.append(cross[0] if power == 3 else cross)
-        moments.append(same)
-        if power == 3:
-            moments.append(cross[1])
-        for a in range(HALO + ROWS, last + 1):
-            carry, _, _ = advance_row(a, carry)
-        if power == 0:
-            both = spread_out(gather_sum(0, 1))
-            shift = both[1] / both[0]
-
-    share(1, 0, gathered(moments))
-    for number in (1, 2, 3):
-        fill_halos(number)
-
     def tracers(t, _):
         advance((0, 1), t)
         return 0
@@ -564,6 +564,9 @@
     lax.fori_loop(0, PAIRS, tracers, 0)
     out_copies = [write_out(0), write_out(1)]
     share(1, 1, gather_sum(1, 0))
+
+    fill_halos(2)
+    fill_halos(3)
 
     def velocities(t, _):
         advance((2, 3), t)

time: 31.5 us -> 31.1 us (0.987)
    pallas_call x1, Pallas kernels: 28.6 us -> 28.2 us  [local(): pl.pallas_call(functools.partial(kernel, sizes), out_shape=[big] * 4 + [s...]
where the time goes in v5:
time: 31.1 us; the launch traced here: 31 us
  Pallas kernels  30.4 us (98%)
  between operations  0.64 us (2%)
    pallas_call x1, Pallas kernels, local(): pl.pallas_call(functools.partial(kernel, sizes), out_shape=[big] * 4 + [s...  28.2 us
    pallas_call x1, Pallas kernels, finish(): pl.pallas_call(finish_kernel, in_specs=[vmem] * 7, out_specs=[hbm] * 5, o...  2.14 us

profile of v5, /device:TPU:0, one launch (start us, length us, event | category | flops | bytes accessed | tf_op | source)
XLA Modules:
  0.0 31.0 jit_solution(18081691086661425228)
XLA Ops:
  0.6 28.2 %ocean_step.1 = (f32[64,4096]{1,0:T(8,128)S(1)}, f32[64,4096]{1,0:T(8,128)S(1)}, f32[64,4096]{1,0:T(8,128)S(1)}, f32[64,4096]{1,0:T(8,128)S(1)}, f32[8,4096]{1,0...) custom-call(f32[64,4096]{1,0:T(8,128)} %bitcast.10, f32[64,4096]{1,0:T(8,128)} %bitcast.11, ...), custom_call_target="tpu_custom_call" | custom-call | tf_op jit(solution)/shard_map/ocean_step/pallas_call | solution.py:689
  28.9 2.1 %finish.1 = (f32[64,4096]{1,0:T(8,128)}, f32[64,4096]{1,0:T(8,128)}, f32[64,4096]{1,0:T(8,128)}, f32[64,4096]{1,0:T(8,128)}, f32[8,4096]{1,0:T(8,128)}) custom-call(f32[64,4096]{1,0:T(8,128)S(1)} %get-tuple-element.17.t_in, f32[64,4096]{1,0:T(8,128)S(1)} %get-tuple-element.18.s_in, f32[64,4096]{1,0:T(8,128)S(1)} %get-tuple-element.19.u_in, ...), custom_call_target="tpu_custom_call" | custom-call | tf_op jit(solution)/shard_map/finish/pallas_call | solution.py:663

commit v6 on v5

--- a/solution.py
+++ b/solution.py
@@ -274,7 +274,7 @@
         z2[t] = src[:, tile(t)] + inside((0,), t) * (1.0 / LEVELS)
         return 0
 
-    lax.fori_loop(0, PAIRS, first_load, 0)
+    lax.fori_loop(0, PAIRS, first_load, 0, unroll=2)
 
     def share(use, group, value):
         phase = 2 * use + group
@@ -336,7 +336,7 @@
     _, _, norm, product = lax.fori_loop(0, PAIRS, split, (zero, zero, zero, zero), unroll=8)
     share(0, 0, gathered([norm, 2.0 * product]))
 
-    for number in (1, 2, 3):
+    for number in (1, 2):
         shift_field(number)
 
     def fill_halos(number):
@@ -418,9 +418,11 @@
     lax.fori_loop(0, PAIRS, whole_load, 0, unroll=16)
     wide_strips(z2, zstrips)
     z_copies = exchange(zstrips, zarrived, z_send, z_recv)
-    for number in (1, 2, 3):
+    for number in (1, 2):
         strip_copies[number] = send_strips(number)
     share(0, 1, gather_sum(0, 0))
+    shift_field(3)
+    strip_copies[3] = send_strips(3)
 
     def others_inside(t, _):
         inside((1, 2, 3), t)

time: 31.1 us -> 30.9 us (level)
  no operation moved by 1% of the time
where the time goes in v6:
time: 30.9 us; the launch traced here: 30.8 us
  Pallas kernels  30.2 us (98%)
  between operations  0.64 us (2%)
    pallas_call x1, Pallas kernels, local(): pl.pallas_call(functools.partial(kernel, sizes), out_shape=[big] * 4 + [s...  28 us
    pallas_call x1, Pallas kernels, finish(): pl.pallas_call(finish_kernel, in_specs=[vmem] * 7, out_specs=[hbm] * 5, o...  2.14 us

profile of v6, /device:TPU:0, one launch (start us, length us, event | category | flops | bytes accessed | tf_op | source)
XLA Modules:
  0.0 30.8 jit_solution(12253110054057473637)
XLA Ops:
  0.6 28.0 %ocean_step.1 = (f32[64,4096]{1,0:T(8,128)S(1)}, f32[64,4096]{1,0:T(8,128)S(1)}, f32[64,4096]{1,0:T(8,128)S(1)}, f32[64,4096]{1,0:T(8,128)S(1)}, f32[8,4096]{1,0...) custom-call(f32[64,4096]{1,0:T(8,128)} %bitcast.10, f32[64,4096]{1,0:T(8,128)} %bitcast.11, ...), custom_call_target="tpu_custom_call" | custom-call | tf_op jit(solution)/shard_map/ocean_step/pallas_call | solution.py:691
  28.7 2.1 %finish.1 = (f32[64,4096]{1,0:T(8,128)}, f32[64,4096]{1,0:T(8,128)}, f32[64,4096]{1,0:T(8,128)}, f32[64,4096]{1,0:T(8,128)}, f32[8,4096]{1,0:T(8,128)}) custom-call(f32[64,4096]{1,0:T(8,128)S(1)} %get-tuple-element.17.t_in, f32[64,4096]{1,0:T(8,128)S(1)} %get-tuple-element.18.s_in, f32[64,4096]{1,0:T(8,128)S(1)} %get-tuple-element.19.u_in, ...), custom_call_target="tpu_custom_call" | custom-call | tf_op jit(solution)/shard_map/finish/pallas_call | solution.py:665
